TPU v7x, 32 devices: a whole 2x2x4 slice. The times are simulated.
32 devices in a mesh: fsdp: 4 (over y, core), ctx: 8 (over z, x).
Axes of the slice: x: 2, y: 2, z: 4, core: 2. Of those that a mesh axis runs over, the one named last changes fastest.
Arguments:
- hidden: bfloat16 [4, 1024, 2048], P('fsdp', 'ctx'), may hold values from -6 to 6
- queries: bfloat16 [4, 1024, 1024], P('fsdp', 'ctx'), may hold values from -6 to 6
- attn_out: bfloat16 [4, 1024, 1024], P('fsdp', 'ctx'), may hold values from -6 to 6
- grad_out: bfloat16 [4, 1024, 1024], P('fsdp', 'ctx'), may hold values from -6 to 6
- log_sums: float32 [4, 16, 1024], P('fsdp', None, 'ctx'), may hold values from 6 to 9
- block_order: int32 [4, 8], P('fsdp'), may hold values from 0 to 7, each once within a row
- w_kv: bfloat16 [2048, 512], P('fsdp'), may hold values from -0.125 to 0.125
Outputs:
- query_grads: bfloat16 [4, 1024, 1024], P('fsdp', 'ctx')
- input_grads: bfloat16 [4, 1024, 2048], P('fsdp', 'ctx')
- weight_grads: float32 [2048, 512], P(('fsdp', 'ctx'))
Inputs may be any that keep to these rules, and one draw needn't show every extreme that they name: Each row of block_order is a permutation of the 8 block numbers.
All inputs are finite; a program needn't handle non-finite values.
Results may differ from a plain program's by a relative error of at most 0.013.
The roundings to bfloat16 on the way count: a program that leaves them out, or rounds other values in their place, can miss the bound.
Values may be sent and summed in bfloat16 or wider, within the bound.
No kernel may reach another device: no remote copies, remote signals or barrier semaphores. Data moves between devices by JAX's collectives and lax.ppermute only.
A program may use at most 128 MiB of HBM per device.

v0:
```python
import functools

import jax
import jax.numpy as jnp
from jax import lax
from jax.experimental import pallas as pl
from jax.experimental.pallas import tpu as pltpu
from jax.sharding import PartitionSpec as P

Q_HEADS = 16
KV_HEADS = 4
HEAD_DIM = 64
GROUPS = Q_HEADS // KV_HEADS
KEY_WIDTH = KV_HEADS * HEAD_DIM
PAIR = 2 * HEAD_DIM
TEAM = 2 * KV_HEADS
GROUP = GROUPS * HEAD_DIM
SCALE = HEAD_DIM ** -0.5
LOWER = HEAD_DIM

NT = (((1,), (1,)), ((), ()))
TN = (((0,), (0,)), ((), ()))
VMEM = pl.BlockSpec(memory_space=pltpu.VMEM)
SMEM = pl.BlockSpec(memory_space=pltpu.SMEM)
ANY = pl.BlockSpec(memory_space=pl.ANY)
HBM = pl.BlockSpec(memory_space=pltpu.HBM)
PARAMS = pltpu.CompilerParams(vmem_limit_bytes=40 * 1024 * 1024)
WHOLE = pltpu.CompilerParams(vmem_limit_bytes=60 * 1024 * 1024)


def matmul(left, right, dims=(((1,), (0,)), ((), ()))):
    return lax.dot_general(left, right, dims, preferred_element_type=jnp.float32)


def swapped(array, axis, bits):
    size = lax.axis_size(axis)
    return lax.ppermute(array, axis, [(i, i ^ bits) for i in range(size)])


def call(kernel, out_shape, scratch, args, smem=0, hbm=0, after=()):
    given = len(args)
    params = WHOLE if hbm else PARAMS

    def body(*refs):
        kernel(*refs[:given], *refs[given + len(after):])

    specs = [SMEM] * smem + [HBM] * hbm + [VMEM] * (given - smem - hbm) + [ANY] * len(after)
    return pl.pallas_call(
        body,
        out_shape=out_shape,
        in_specs=specs,
        out_specs=[VMEM] * len(out_shape),
        scratch_shapes=scratch,
        compiler_params=params,
    )(*args, *after)


def held(array, after):
    def body(*refs):
        pass

    return pl.pallas_call(
        body,
        out_shape=sds(array.shape, array.dtype),
        in_specs=[ANY] * (1 + len(after)),
        out_specs=ANY,
        input_output_aliases={0: 0},
        compiler_params=PARAMS,
    )(array, *after)


def sds(shape, dtype=jnp.bfloat16):
    return jax.ShapeDtypeStruct(shape, dtype)


def head_side():
    me = lax.rem(lax.axis_index("ctx"), TEAM)
    return me // 2, lax.rem(me, 2)


def split(exact):
    first = exact.astype(jnp.bfloat16).astype(jnp.float32)
    second = (exact - first).astype(jnp.bfloat16).astype(jnp.float32)
    return first, second, exact - first - second


def pieces_kernel(q_ref, go_ref, ao_ref, lse_ref, *rest):
    out_refs, (grad, output, lse, stat, sems) = rest[:KV_HEADS], rest[KV_HEADS:]
    rows, width = q_ref.shape
    head, _ = head_side()
    loads = [pltpu.make_async_copy(ref, to, sems.at[i])
             for i, (ref, to) in enumerate(((go_ref, grad), (ao_ref, output), (lse_ref, lse)))]
    moves = []
    for m in range(KV_HEADS):
        columns = pl.ds(pl.multiple_of(jnp.bitwise_xor(head, m) * GROUP, GROUP), GROUP)
        for i, ref in enumerate((q_ref, go_ref)):
            moves.append(pltpu.make_async_copy(
                ref.at[:, columns], out_refs[m].at[0:rows, i * GROUP:(i + 1) * GROUP], sems.at[3 + 2 * m + i]))
    for copy in loads + moves:
        copy.start()
    for copy in loads:
        copy.wait()
    product = grad[...].astype(jnp.float32) * output[...].astype(jnp.float32)
    high = product.astype(jnp.bfloat16)
    low = (product - high.astype(jnp.float32)).astype(jnp.bfloat16)
    head_of = lax.broadcasted_iota(jnp.int32, (Q_HEADS, width), 1) // HEAD_DIM
    ones = (head_of == lax.broadcasted_iota(jnp.int32, (Q_HEADS, width), 0)).astype(jnp.bfloat16)
    delta = matmul(ones, high, NT) + matmul(ones, low, NT)
    for g in range(KV_HEADS):
        part = slice(g * GROUPS, (g + 1) * GROUPS)
        stat[g] = jnp.concatenate([lse[part, :], delta[part, :]], axis=0)
    zero = jnp.zeros((2 * GROUPS, rows), jnp.float32)
    for m in range(KV_HEADS):
        lines = [*split(stat[jnp.bitwise_xor(head, m)]), zero]
        for i, one in enumerate(lines):
            full = jnp.concatenate([one, zero], axis=0).astype(jnp.bfloat16)
            out_refs[m][rows:, i * rows:(i + 1) * rows] = full
    for copy in moves:
        copy.wait()


def hidden_kernel(fsdp, hid_ref, *rest):
    near_refs, far_ref, sems = rest[:fsdp // 2], rest[fsdp // 2], rest[fsdp // 2 + 1]
    mine = lax.axis_index("fsdp")
    span = far_ref.shape[2]
    copies = []
    for m in range(fsdp):
        columns = pl.ds(pl.multiple_of(jnp.bitwise_xor(mine, m) * span, span), span)
        to = near_refs[m] if m < fsdp // 2 else far_ref.at[m - fsdp // 2]
        copies.append(pltpu.make_async_copy(hid_ref.at[:, columns], to, sems.at[m]))
    for copy in copies:
        copy.start()
    for copy in copies:
        copy.wait()


def project_kernel(fsdp, hid_ref, *rest):
    w_refs, out_refs, (parts,) = rest[:fsdp], rest[fsdp:fsdp + KV_HEADS], rest[fsdp + KV_HEADS:]
    mine = lax.axis_index("fsdp")
    head, _ = head_side()
    span = w_refs[0].shape[0]
    total = None
    for m in range(fsdp):
        start = pl.multiple_of(jnp.bitwise_xor(mine, m) * span, span)
        term = matmul(hid_ref[:, pl.ds(start, span)], w_refs[m][...])
        total = term if total is None else total + term
    low = total.astype(jnp.bfloat16)
    for g in range(KV_HEADS):
        key = low[:, g * HEAD_DIM:(g + 1) * HEAD_DIM]
        value = low[:, KEY_WIDTH + g * HEAD_DIM:KEY_WIDTH + (g + 1) * HEAD_DIM]
        parts[g] = jnp.concatenate([key, value], axis=1)
    for m in range(KV_HEADS):
        out_refs[m][...] = parts[jnp.bitwise_xor(head, m)]


def lower_half(shape):
    return lax.broadcasted_iota(jnp.int32, shape, len(shape) - 1) < LOWER


def stacked(key_value):
    wide = key_value.astype(jnp.float32)
    turned = pltpu.roll(wide, LOWER, 1)
    lower = lower_half(wide.shape)
    zero = jnp.zeros_like(wide)
    keys = jnp.concatenate([jnp.where(lower, wide, zero), jnp.where(lower, zero, turned)], axis=0) * SCALE
    values = jnp.concatenate([jnp.where(lower, turned, zero), jnp.where(lower, zero, wide)], axis=0)
    return keys.astype(jnp.bfloat16), values.astype(jnp.bfloat16)


def tile(keys, values, query, grad, stats, mask):
    size = keys.shape[0] // 2
    lse, delta = stats[:2], stats[2:]
    scores = matmul(keys, query, NT)
    prob_grad = matmul(values, grad, NT)
    lows, grads = [], []
    for head in range(2):
        part = slice(head * size, (head + 1) * size)
        probs = jnp.exp(scores[part] - lse[head])
        if mask is not None:
            probs = jnp.where(mask, probs, 0.0)
        lows.append(probs.astype(jnp.bfloat16))
        grads.append((probs * (prob_grad[part] - delta[head])).astype(jnp.bfloat16))
    low, score_grad = jnp.concatenate(lows, axis=0), jnp.concatenate(grads, axis=0)
    return matmul(score_grad, query), matmul(low, grad), matmul(score_grad, keys, TN)


def folded(key_sum, value_sum):
    size = key_sum.shape[0] // 2
    lower = lower_half((size, PAIR))
    straight = jnp.where(lower, key_sum[:size], value_sum[size:])
    crossed = jnp.where(lower, value_sum[:size], key_sum[size:])
    return (straight + pltpu.roll(crossed, LOWER, 1)) * jnp.where(lower, SCALE, 1.0)


def unpacked(part, rows):
    exact = part[rows:, 0:3 * rows].astype(jnp.float32)[0:2 * GROUPS]
    return exact[:, 0:rows] + exact[:, rows:2 * rows] + exact[:, 2 * rows:]


def pair_stats(stat, pair):
    first = 2 * pair
    return [stat[first:first + 1], stat[first + 1:first + 2],
            stat[GROUPS + first:GROUPS + first + 1], stat[GROUPS + first + 1:GROUPS + first + 2]]


def sequence_kernel(order_ref, *rest):
    qd_refs, kv_refs, rest = rest[:TEAM], rest[TEAM:TEAM + KV_HEADS], rest[TEAM + KV_HEADS:]
    dkv_refs, keep_ref, send_ref, rest = rest[:KV_HEADS], rest[KV_HEADS], rest[KV_HEADS + 1], rest[KV_HEADS + 2:]
    q_all, go_all, stat_all, key_all, value_all, dq_all, dkv_all = rest
    rows = kv_refs[0].shape[0]
    head, side = head_side()
    near = [order_ref[0, 2 * jnp.bitwise_xor(head, m) + side] for m in range(KV_HEADS)]
    far = [order_ref[0, 2 * jnp.bitwise_xor(head, m) + 1 - side] for m in range(KV_HEADS)]
    for place, ref in zip(near + far, qd_refs):
        q_all[place] = ref[0:rows, 0:GROUP]
        go_all[place] = ref[0:rows, GROUP:]
        stat_all[place] = unpacked(ref, rows)
    for place, ref in zip(near, kv_refs):
        key_all[place], value_all[place] = stacked(ref[...])
    dq_all[...] = jnp.zeros_like(dq_all)
    for block in range(TEAM):
        mine = functools.reduce(jnp.logical_or, [place == block for place in near])

        @pl.when(mine)
        def _():
            count = TEAM - block
            shape = (rows, count * rows)
            mask = lax.broadcasted_iota(jnp.int32, shape, 0) <= lax.broadcasted_iota(jnp.int32, shape, 1)
            stats = jnp.concatenate([stat_all[i] for i in range(block, TEAM)], axis=1)
            key_sum = value_sum = None
            for pair in range(GROUPS // 2):
                columns = slice(pair * PAIR, (pair + 1) * PAIR)
                query = q_all[block:, :, columns].reshape(count * rows, PAIR)
                grad = go_all[block:, :, columns].reshape(count * rows, PAIR)
                key_part, value_part, query_part = tile(
                    key_all[block], value_all[block], query, grad, pair_stats(stats, pair), mask)
                key_sum = key_part if key_sum is None else key_sum + key_part
                value_sum = value_part if value_sum is None else value_sum + value_part
                dq_all[block:, :, columns] += query_part.reshape(count, rows, PAIR)
            dkv_all[block] = folded(key_sum, value_sum)

    for m in range(KV_HEADS):
        dkv_refs[m][...] = dkv_all[near[m]].astype(jnp.bfloat16)
        keep_ref[m] = dq_all[near[m]]
        send_ref[m] = dq_all[far[m]].astype(jnp.bfloat16)


def teams_kernel(order_ref, qd_ref, kv_ref, dkv_ref, keep_ref, send_ref, dq_all):
    rows = kv_ref.shape[1]
    head, side = head_side()
    base = lax.axis_index("ctx") // TEAM * TEAM
    dq_all[...] = jnp.zeros_like(dq_all)

    @pl.loop(0, kv_ref.shape[0])
    def _(block):
        keys, values = stacked(kv_ref[block])
        dkv_ref[block] = jnp.zeros((rows, PAIR), jnp.float32)
        stored = block // KV_HEADS * TEAM + 2 * jnp.bitwise_xor(head, lax.rem(block, KV_HEADS)) + side
        place = order_ref[0, stored]

        @pl.loop(0, TEAM)
        def _(at):
            turned = jnp.where(at < KV_HEADS, side, 1 - side)
            own = order_ref[0, base + 2 * jnp.bitwise_xor(head, lax.rem(at, KV_HEADS)) + turned]

            @pl.when(place <= own)
            def _():
                shape = (rows, rows)
                mask = (place * rows + lax.broadcasted_iota(jnp.int32, shape, 0)
                        <= own * rows + lax.broadcasted_iota(jnp.int32, shape, 1))
                one = qd_ref.at[at]
                stats = unpacked(one, rows)
                for pair in range(GROUPS // 2):
                    first = pair * PAIR
                    key_part, value_part, query_part = tile(
                        keys, values, one[0:rows, first:first + PAIR], one[0:rows, GROUP + first:GROUP + first + PAIR],
                        pair_stats(stats, pair), mask)
                    dq_all[at, :, first:first + PAIR] += query_part
                    dkv_ref[block] += folded(key_part, value_part)

    keep_ref[...] = dq_all[0:KV_HEADS]
    send_ref[...] = dq_all[KV_HEADS:].astype(jnp.bfloat16)


def owner_kernel(*rest):
    dkv_refs, out_ref, parts = rest[:KV_HEADS], rest[KV_HEADS], rest[KV_HEADS + 1]
    head, _ = head_side()
    for m in range(KV_HEADS):
        parts[jnp.bitwise_xor(head, m)] = dkv_refs[m][...]
    keys = [parts[g, :, :HEAD_DIM] for g in range(KV_HEADS)]
    values = [parts[g, :, HEAD_DIM:] for g in range(KV_HEADS)]
    out_ref[...] = jnp.concatenate(keys + values, axis=1)


def pair_kernel(keep_ref, got_ref, *out_refs):
    for m in range(KV_HEADS):
        out_refs[m][...] = (keep_ref[m] + got_ref[m].astype(jnp.float32)).astype(jnp.bfloat16)


def query_kernel(*rest):
    dq_refs, out_ref = rest[:KV_HEADS], rest[KV_HEADS]
    head, _ = head_side()
    for m in range(KV_HEADS):
        columns = pl.ds(pl.multiple_of(jnp.bitwise_xor(head, m) * GROUP, GROUP), GROUP)
        out_ref[:, columns] = dq_refs[m][...]


def input_kernel(fsdp, grad_ref, *rest):
    w_refs, out_ref = rest[:fsdp], rest[fsdp]
    mine = lax.axis_index("fsdp")
    span = w_refs[0].shape[0]
    for m in range(fsdp):
        start = pl.multiple_of(jnp.bitwise_xor(mine, m) * span, span)
        out_ref[:, pl.ds(start, span)] = matmul(grad_ref[...], w_refs[m][...], NT).astype(jnp.bfloat16)


def weight_kernel(fsdp, *rest):
    hid_refs, grad_refs, out_ref = rest[:fsdp], rest[fsdp:2 * fsdp], rest[2 * fsdp]
    hid = jnp.concatenate([ref[...] for ref in hid_refs], axis=0)
    grad = jnp.concatenate([ref[...] for ref in grad_refs], axis=0)
    out_ref[...] = matmul(hid, grad, TN).astype(jnp.bfloat16)


def total_kernel(part_ref, out_ref):
    total = part_ref[0].astype(jnp.float32)
    for i in range(1, part_ref.shape[0]):
        total = total + part_ref[i].astype(jnp.float32)
    out_ref[...] = total


def over_fsdp(own, bits):
    got = list(own)
    while bits:
        for m in range(len(own)):
            if m & bits:
                got[m] = swapped(got[m], "fsdp", bits)
        bits //= 2
    return got


def shards(hidden, queries, attn_out, grad_out, log_sums, block_order, w_kv):
    rows, model = hidden.shape[1:]
    fsdp, devices = lax.axis_size("fsdp"), lax.axis_size("ctx")
    teams = devices // TEAM
    f32 = jnp.float32
    span = model // fsdp
    inputs = hidden[0]
    columns = 2 * KEY_WIDTH
    block, wide = (rows, PAIR), (rows, GROUP)

    def along_heads(arrays):
        return [arrays[0]] + [swapped(arrays[m], "ctx", 2 * m) for m in range(1, KV_HEADS)]

    far = fsdp // 2
    qd = call(
        pieces_kernel, [sds((rows + 16, 2 * GROUP))] * KV_HEADS,
        [pltpu.VMEM((rows, Q_HEADS * HEAD_DIM), jnp.bfloat16)] * 2
        + [pltpu.VMEM((Q_HEADS, rows), f32), pltpu.VMEM((KV_HEADS, 2 * GROUPS, rows), f32),
           pltpu.SemaphoreType.DMA((3 + 2 * KV_HEADS,))],
        (queries[0], grad_out[0], attn_out[0], log_sums[0]), hbm=4)
    qd = along_heads(qd)
    qd = qd + [swapped(one, "ctx", 1) for one in qd]
    w_far = held(swapped(w_kv, "fsdp", far), (qd[1], qd[2], qd[KV_HEADS]))
    w_parts = over_fsdp([w_kv] * far + [w_far] * (fsdp - far), far // 2)

    kv = call(
        functools.partial(project_kernel, fsdp), [sds(block)] * KV_HEADS,
        [pltpu.VMEM((KV_HEADS,) + block, jnp.bfloat16)], (inputs, *w_parts), after=(*qd[1:KV_HEADS], qd[KV_HEADS]))
    kv = along_heads(kv)

    *hid, hid_far = call(
        functools.partial(hidden_kernel, fsdp), [sds((rows, span))] * far + [sds((fsdp - far, rows, span))],
        [pltpu.SemaphoreType.DMA((fsdp,))], (inputs,), hbm=1)
    hid_far = swapped(hid_far, "fsdp", far)
    hid = over_fsdp(hid + [hid_far[m] for m in range(fsdp - far)], far // 2)

    half = (KV_HEADS,) + wide
    if teams == 1:
        *dkv, keep, give = call(
            sequence_kernel, [sds(block)] * KV_HEADS + [sds(half, f32), sds(half)],
            [pltpu.VMEM((TEAM,) + wide, jnp.bfloat16)] * 2 + [pltpu.VMEM((TEAM, 2 * GROUPS, rows), f32)]
            + [pltpu.VMEM((TEAM, 2 * rows, PAIR), jnp.bfloat16)] * 2
            + [pltpu.VMEM((TEAM,) + wide, f32), pltpu.VMEM((TEAM,) + block, f32)],
            (block_order, *qd, *kv), smem=1, after=hid[1:])
    else:
        alike = [[t * TEAM + i for t in range(teams)] for i in range(TEAM)]
        kv = lax.all_gather(jnp.stack(kv), "ctx", axis_index_groups=alike, axis=0, tiled=True)
        dkv, keep, give = call(
            teams_kernel, [sds((teams * KV_HEADS,) + block, f32), sds(half, f32), sds(half)],
            [pltpu.VMEM((TEAM,) + wide, f32)], (block_order, jnp.stack(qd), kv), smem=1)
        dkv = lax.psum_scatter(dkv, "ctx", axis_index_groups=alike, scatter_dimension=0, tiled=True)
        dkv = [dkv[m].astype(jnp.bfloat16) for m in range(KV_HEADS)]

    give = swapped(give, "ctx", 1)
    (kv_grad,) = call(
        owner_kernel, [sds((rows, columns))], [pltpu.VMEM((KV_HEADS,) + block, jnp.bfloat16)],
        along_heads(dkv), after=(give,))
    grads = over_fsdp([kv_grad] * fsdp, far)
    (parts,) = call(functools.partial(weight_kernel, fsdp), [sds((span, columns))], [], (*hid, *grads))
    sums = lax.all_to_all(parts.reshape(devices, span // devices, columns), "ctx", 0, 0, tiled=True)

    dq = call(pair_kernel, [sds(wide)] * KV_HEADS, [], (keep, give))
    (query_grads,) = call(query_kernel, [sds((rows, Q_HEADS * HEAD_DIM))], [], along_heads(dq), after=(parts,))
    (input_grads,) = call(functools.partial(input_kernel, fsdp), [sds((rows, model))], [], (kv_grad, *w_parts), after=(parts,))
    (weight_grads,) = call(total_kernel, [sds((span // devices, columns), f32)], [], (sums,))
    return query_grads[None], input_grads[None], weight_grads


def solution(mesh):
    return jax.shard_map(
        shards,
        mesh=mesh,
        in_specs=(
            P("fsdp", "ctx", None),
            P("fsdp", "ctx", None),
            P("fsdp", "ctx", None),
            P("fsdp", "ctx", None),
            P("fsdp", None, "ctx"),
            P("fsdp", None),
            P("fsdp", None),
        ),
        out_specs=(P("fsdp", "ctx", None), P("fsdp", "ctx", None), P(("fsdp", "ctx"), None)),
        check_vma=False,
    )
```

profile of v0, /device:TPU:0, one launch (start us, length us, event | category | flops | bytes accessed | tf_op | source)
XLA Modules:
  0.0 94.1 jit_solution(7349798333946382729)
XLA Ops:
  0.6 3.0 %collective-permute-start.8 = (bf16[512,512]{1,0:T(8,128)(2,1)}, bf16[512,512]{1,0:T(8,128)(2,1)S(1)}, u32[]{:S(2)}, u32[]{:S(2)}) collective-permute-start(bf16[512,512]{1,0:T(8,128)(2,1)} %refs_1_.3), channel_id=1, source_target_pairs={{0,16},{8,24},{16,0},{24,8},{1,17},{9,25},{17,1},{25,9},{2,18},{10... | collective-permute-start | bytes 1572872 | tf_op jit(solution)/shard_map/ppermute | solution.py:37
  3.7 2.2 %shard_map.94 = (bf16[144,512]{1,0:T(8,128)(2,1)}, bf16[144,512]{1,0:T(8,128)(2,1)}, bf16[144,512]{1,0:T(8,128)(2,1)}, bf16[144,512]{1,0:T(8,128)(2,1)}) custom-call(bf16[128,1024]{1,0:T(8,128)(2,1)} %bitcast.15, bf16[128,1024]{1,0:T(8,128)(2,1)} %bitcast.16, bf16[128,1024]{1,0:T(8,128)(2,1)} %bitcast.17, f32[16,128]{1,0:T(8,128)} %bitcast.19), custom_call_target="tpu_custom_call" | custom-call | tf_op jit(solution)/shard_map/pallas_call | solution.py:48
  5.9 1.6 %collective-permute-start = (bf16[144,512]{1,0:T(8,128)(2,1)}, bf16[144,512]{1,0:T(8,128)(2,1)S(1)}, u32[]{:S(2)}, u32[]{:S(2)}) collective-permute-start(bf16[144,512]{1,0:T(8,128)(2,1)} %get-tuple-element.25), channel_id=1, source_target_pairs={{0,2},{1,3},{2,0},{3,1},{4,6},{5,7},{6,4},{7,5},{8,10},{9,11},{10,... | collective-permute-start | bytes 442376 | tf_op jit(solution)/shard_map/ppermute | solution.py:37
  7.5 2.6 %collective-permute-start.1 = (bf16[144,512]{1,0:T(8,128)(2,1)}, bf16[144,512]{1,0:T(8,128)(2,1)S(1)}, u32[]{:S(2)}, u32[]{:S(2)}) collective-permute-start(bf16[144,512]{1,0:T(8,128)(2,1)} %get-tuple-element.26), channel_id=1, source_target_pairs={{0,4},{1,5},{2,6},{3,7},{4,0},{5,1},{6,2},{7,3},{8,12},{9,13},{10,... | collective-permute-start | bytes 442376 | tf_op jit(solution)/shard_map/ppermute | solution.py:37
  10.1 1.5 %collective-permute-start.3 = (bf16[144,512]{1,0:T(8,128)(2,1)}, bf16[144,512]{1,0:T(8,128)(2,1)S(1)}, u32[]{:S(2)}, u32[]{:S(2)}) collective-permute-start(bf16[144,512]{1,0:T(8,128)(2,1)} %get-tuple-element.24.refs_1_), channel_id=1, source_target_pairs={{0,1},{1,0},{2,3},{3,2},{4,5},{5,4},{6,7},{7,6},{8,9},{9,8},{10,11... | collective-permute-start | bytes 442376 | tf_op jit(solution)/shard_map/ppermute | solution.py:37
  11.6 3.9 %collective-permute-done.refs_1_.refs_5_.refs_2_ = bf16[144,512]{1,0:T(8,128)(2,1)S(1)} collective-permute-done((bf16[144,512]{1,0:T(8,128)(2,1)}, bf16[144,512]{1,0:T(8,128)(2,1)S(1)}, u32[]{:S(2)}, u32[]{:S(2)}) %collective-permute-start) | collective-permute-done | bytes 147488 | tf_op jit(solution)/shard_map/ppermute | solution.py:37
  15.5 2.4 %collective-permute-done.1.refs_2_.refs_6_.refs_3_ = bf16[144,512]{1,0:T(8,128)(2,1)S(1)} collective-permute-done((bf16[144,512]{1,0:T(8,128)(2,1)}, bf16[144,512]{1,0:T(8,128)(2,1)S(1)}, u32[]{:S(2)}, u32[]{:S(2)}) %collective-permute-start.1) | collective-permute-done | bytes 147488 | tf_op jit(solution)/shard_map/ppermute | solution.py:37
  18.0 2.0 %shard_map.97 = (bf16[128,512]{1,0:T(8,128)(2,1)}, bf16[128,512]{1,0:T(8,128)(2,1)}, bf16[2,128,512]{2,1,0:T(8,128)(2,1)}) custom-call(bf16[128,2048]{1,0:T(8,128)(2,1)} %bitcast.12), custom_call_target="tpu_custom_call" | custom-call | tf_op jit(solution)/shard_map/pallas_call | solution.py:48
  20.6 2.7 %collective-permute-start.2 = (bf16[144,512]{1,0:T(8,128)(2,1)S(1)}, bf16[144,512]{1,0:T(8,128)(2,1)S(1)}, u32[]{:S(2)}, u32[]{:S(2)}) collective-permute-start(bf16[144,512]{1,0:T(8,128)(2,1)S(1)} %copy-done.5), channel_id=1, source_target_pairs={{0,6},{1,7},{2,4},{3,5},{4,2},{5,3},{6,0},{7,1},{8,14},{9,15},{10,... | collective-permute-start | bytes 442376 | tf_op jit(solution)/shard_map/ppermute | solution.py:37
  23.3 5.1 %collective-permute-done.2.refs_7_.refs_4_ = bf16[144,512]{1,0:T(8,128)(2,1)S(1)} collective-permute-done((bf16[144,512]{1,0:T(8,128)(2,1)S(1)}, bf16[144,512]{1,0:T(8,128)(2,1)S(1)}, u32[]{:S(2)}, u32[]{:S(2)}) %collective-permute-start.2) | collective-permute-done | bytes 147488 | tf_op jit(solution)/shard_map/ppermute | solution.py:37
  28.4 1.5 %collective-permute-start.4 = (bf16[144,512]{1,0:T(8,128)(2,1)S(1)}, bf16[144,512]{1,0:T(8,128)(2,1)S(1)}, u32[]{:S(2)}, u32[]{:S(2)}) collective-permute-start(bf16[144,512]{1,0:T(8,128)(2,1)S(1)} %collective-permute-done.refs_1_.refs_5_.refs_2_), channel_id=1, source_target_pairs={{0,1},{1,0},{2,3},{3,2},{4,5},{5,4},{6,7},{7,6},{8,9},{9,8},{10,11... | collective-permute-start | bytes 442376 | tf_op jit(solution)/shard_map/ppermute | solution.py:37
  30.4 1.5 %collective-permute-start.6 = (bf16[144,512]{1,0:T(8,128)(2,1)S(1)}, bf16[144,512]{1,0:T(8,128)(2,1)S(1)}, u32[]{:S(2)}, u32[]{:S(2)}) collective-permute-start(bf16[144,512]{1,0:T(8,128)(2,1)S(1)} %collective-permute-done.2.refs_7_.refs_4_), channel_id=1, source_target_pairs={{0,1},{1,0},{2,3},{3,2},{4,5},{5,4},{6,7},{7,6},{8,9},{9,8},{10,11... | collective-permute-start | bytes 442376 | tf_op jit(solution)/shard_map/ppermute | solution.py:37
  32.6 2.0 %collective-permute-start.10 = (bf16[128,128]{1,0:T(8,128)(2,1)S(1)}, bf16[128,128]{1,0:T(8,128)(2,1)S(1)}, u32[]{:S(2)}, u32[]{:S(2)}) collective-permute-start(bf16[128,128]{1,0:T(8,128)(2,1)S(1)} %get-tuple-element.29), channel_id=1, source_target_pairs={{0,2},{1,3},{2,0},{3,1},{4,6},{5,7},{6,4},{7,5},{8,10},{9,11},{10,... | collective-permute-start | bytes 98312 | tf_op jit(solution)/shard_map/ppermute | solution.py:37
  35.2 3.0 %collective-permute-start.11 = (bf16[128,128]{1,0:T(8,128)(2,1)S(1)}, bf16[128,128]{1,0:T(8,128)(2,1)S(1)}, u32[]{:S(2)}, u32[]{:S(2)}) collective-permute-start(bf16[128,128]{1,0:T(8,128)(2,1)S(1)} %get-tuple-element.30), channel_id=1, source_target_pairs={{0,4},{1,5},{2,6},{3,7},{4,0},{5,1},{6,2},{7,3},{8,12},{9,13},{10,... | collective-permute-start | bytes 98312 | tf_op jit(solution)/shard_map/ppermute | solution.py:37
  38.2 2.7 %collective-permute-start.12 = (bf16[128,128]{1,0:T(8,128)(2,1)S(1)}, bf16[128,128]{1,0:T(8,128)(2,1)S(1)}, u32[]{:S(2)}, u32[]{:S(2)}) collective-permute-start(bf16[128,128]{1,0:T(8,128)(2,1)S(1)} %get-tuple-element.31), channel_id=1, source_target_pairs={{0,6},{1,7},{2,4},{3,5},{4,2},{5,3},{6,0},{7,1},{8,14},{9,15},{10,... | collective-permute-start | bytes 98312 | tf_op jit(solution)/shard_map/ppermute | solution.py:37
  40.9 3.0 %collective-permute-done.12.refs_12_ = bf16[128,128]{1,0:T(8,128)(2,1)S(1)} collective-permute-done((bf16[128,128]{1,0:T(8,128)(2,1)S(1)}, bf16[128,128]{1,0:T(8,128)(2,1)S(1)}, u32[]{:S(2)}, u32[]{:S(2)}) %collective-permute-start.12) | collective-permute-done | bytes 32800 | tf_op jit(solution)/shard_map/ppermute | solution.py:37
  44.6 5.1 %shard_map.98 = (bf16[128,128]{1,0:T(8,128)(2,1)S(1)}, bf16[128,128]{1,0:T(8,128)(2,1)S(1)}, bf16[128,128]{1,0:T(8,128)(2,1)S(1)}, bf16[128,128]{1,0:T(8,128)(2,...) custom-call(s32[1,8]{1,0:T(1,128)S(1)} %copy-done.4, bf16[144,512]{1,0:T(8,128)(2,1)S(1)} %copy-done.2, ...), custom_call_target="tpu_custom_call" | custom-call | tf_op jit(solution)/shard_map/pallas_call | solution.py:48
  49.7 2.8 %collective-permute-start.16 = (bf16[4,128,256]{2,1,0:T(8,128)(2,1)S(1)}, bf16[4,128,256]{2,1,0:T(8,128)(2,1)S(1)}, u32[]{:S(2)}, u32[]{:S(2)}) collective-permute-start(bf16[4,128,256]{2,1,0:T(8,128)(2,1)S(1)} %get-tuple-element.35), channel_id=1, source_target_pairs={{0,1},{1,0},{2,3},{3,2},{4,5},{5,4},{6,7},{7,6},{8,9},{9,8},{10,11... | collective-permute-start | bytes 786440 | tf_op jit(solution)/shard_map/ppermute | solution.py:37
  52.6 3.1 %collective-permute-start.21 = (bf16[128,128]{1,0:T(8,128)(2,1)S(1)}, bf16[128,128]{1,0:T(8,128)(2,1)S(1)}, u32[]{:S(2)}, u32[]{:S(2)}) collective-permute-start(bf16[128,128]{1,0:T(8,128)(2,1)S(1)} %get-tuple-element.43), channel_id=1, source_target_pairs={{0,4},{1,5},{2,6},{3,7},{4,0},{5,1},{6,2},{7,3},{8,12},{9,13},{10,... | collective-permute-start | bytes 98312 | tf_op jit(solution)/shard_map/ppermute | solution.py:37
  55.7 1.1 %collective-permute-start.22 = (bf16[128,128]{1,0:T(8,128)(2,1)S(1)}, bf16[128,128]{1,0:T(8,128)(2,1)S(1)}, u32[]{:S(2)}, u32[]{:S(2)}) collective-permute-start(bf16[128,128]{1,0:T(8,128)(2,1)S(1)} %get-tuple-element.44), channel_id=1, source_target_pairs={{0,6},{1,7},{2,4},{3,5},{4,2},{5,3},{6,0},{7,1},{8,14},{9,15},{10,... | collective-permute-start | bytes 98312 | tf_op jit(solution)/shard_map/ppermute | solution.py:37
  56.8 0.8 collective-permute-done.21.refs_2_
  57.6 3.8 %collective-permute-done.22.refs_3_ = bf16[128,128]{1,0:T(8,128)(2,1)S(1)} collective-permute-done((bf16[128,128]{1,0:T(8,128)(2,1)S(1)}, bf16[128,128]{1,0:T(8,128)(2,1)S(1)}, u32[]{:S(2)}, u32[]{:S(2)}) %collective-permute-start.22) | collective-permute-done | bytes 32800 | tf_op jit(solution)/shard_map/ppermute | solution.py:37
  61.5 1.1 %collective-permute-start.24 = (bf16[128,512]{1,0:T(8,128)(2,1)S(1)}, bf16[128,512]{1,0:T(8,128)(2,1)S(1)}, u32[]{:S(2)}, u32[]{:S(2)}) collective-permute-start(bf16[128,512]{1,0:T(8,128)(2,1)S(1)} %shard_map.100.refs_4_.refs_0_), channel_id=1, source_target_pairs={{0,16},{8,24},{16,0},{24,8},{1,17},{9,25},{17,1},{25,9},{2,18},{10... | collective-permute-start | bytes 393224 | tf_op jit(solution)/shard_map/ppermute | solution.py:37
  62.7 3.9 %collective-permute-done.24.refs_6_ = bf16[128,512]{1,0:T(8,128)(2,1)S(1)} collective-permute-done((bf16[128,512]{1,0:T(8,128)(2,1)S(1)}, bf16[128,512]{1,0:T(8,128)(2,1)S(1)}, u32[]{:S(2)}, u32[]{:S(2)}) %collective-permute-start.24) | collective-permute-done | bytes 131104 | tf_op jit(solution)/shard_map/ppermute | solution.py:37
  66.6 1.3 %collective-permute-done.25.refs_7_ = bf16[128,512]{1,0:T(8,128)(2,1)S(1)} collective-permute-done((bf16[128,512]{1,0:T(8,128)(2,1)S(1)}, bf16[128,512]{1,0:T(8,128)(2,1)S(1)}, u32[]{:S(2)}, u32[]{:S(2)}) %collective-permute-start.25) | collective-permute-done | bytes 131104 | tf_op jit(solution)/shard_map/ppermute | solution.py:37
  67.9 1.3 %shard_map.101.refs_4_.refs_5_ = bf16[512,512]{1,0:T(8,128)(2,1)} custom-call(bf16[128,512]{1,0:T(8,128)(2,1)S(1)} %copy-done.3, bf16[128,512]{1,0:T(8,128)(2,1)S(1)} %collective-permute-done.13.refs_13_.refs_1_, bf16[128,512]{1,0:T(8,128)(2,1)S(1)} %get-tuple-element.46.refs_14_.refs_2_, bf16[128,512]{1,0:T(8,128)(2,1)S(1)} %collective-permute-done.15.refs_15_.refs_3_, ...), custom_call_target="tpu_custom_call" | custom-call | tf_op jit(solution)/shard_map/pallas_call | solution.py:48
  69.2 3.5 %all-to-all-start = ((bf16[8,64,512]{2,1,0:T(8,128)(2,1)}), bf16[8,64,512]{2,1,0:T(8,128)(2,1)S(1)}, u32[]{:S(2)}, u32[]{:S(2)}) async-start(bf16[8,64,512]{2,1,0:T(8,128)(2,1)} %bitcast.9), calls=%async_computation | async-start | bytes 1048576 | tf_op jit(solution)/shard_map/all_to_all | solution.py:400
  72.8 2.0 %collective-permute-start.17 = (bf16[128,256]{1,0:T(8,128)(2,1)S(1)}, bf16[128,256]{1,0:T(8,128)(2,1)S(1)}, u32[]{:S(2)}, u32[]{:S(2)}) collective-permute-start(bf16[128,256]{1,0:T(8,128)(2,1)S(1)} %get-tuple-element.37), channel_id=1, source_target_pairs={{0,2},{1,3},{2,0},{3,1},{4,6},{5,7},{6,4},{7,5},{8,10},{9,11},{10,... | collective-permute-start | bytes 196616 | tf_op jit(solution)/shard_map/ppermute | solution.py:37
  74.8 2.4 %collective-permute-start.18 = (bf16[128,256]{1,0:T(8,128)(2,1)S(1)}, bf16[128,256]{1,0:T(8,128)(2,1)S(1)}, u32[]{:S(2)}, u32[]{:S(2)}) collective-permute-start(bf16[128,256]{1,0:T(8,128)(2,1)S(1)} %get-tuple-element.38), channel_id=1, source_target_pairs={{0,4},{1,5},{2,6},{3,7},{4,0},{5,1},{6,2},{7,3},{8,12},{9,13},{10,... | collective-permute-start | bytes 196616 | tf_op jit(solution)/shard_map/ppermute | solution.py:37
  77.2 1.6 %shard_map.103 = bf16[128,2048]{1,0:T(8,128)(2,1)} custom-call(bf16[128,512]{1,0:T(8,128)(2,1)S(1)} %shard_map.100.refs_4_.refs_0_, bf16[512,512]{1,0:T(8,128)(2,1)S(1)} %copy-done, bf16[512,512]{1,0:T(8,128)(2,1)S(1)} %collective-permute-done.7.refs_2_, bf16[512,512]{1,0:T(8,128)(2,1)S(1)} %shard_map.95.refs_3_, ...), custom_call_target="tpu_custom_call" | custom-call | tf_op jit(solution)/shard_map/pallas_call | solution.py:48
  78.8 4.9 %collective-permute-done.17.refs_1_ = bf16[128,256]{1,0:T(8,128)(2,1)S(1)} collective-permute-done((bf16[128,256]{1,0:T(8,128)(2,1)S(1)}, bf16[128,256]{1,0:T(8,128)(2,1)S(1)}, u32[]{:S(2)}, u32[]{:S(2)}) %collective-permute-start.17) | collective-permute-done | bytes 65568 | tf_op jit(solution)/shard_map/ppermute | solution.py:37
  83.7 8.9 %collective-permute-done.18.refs_2_ = bf16[128,256]{1,0:T(8,128)(2,1)S(1)} collective-permute-done((bf16[128,256]{1,0:T(8,128)(2,1)S(1)}, bf16[128,256]{1,0:T(8,128)(2,1)S(1)}, u32[]{:S(2)}, u32[]{:S(2)}) %collective-permute-start.18) | collective-permute-done | bytes 65568 | tf_op jit(solution)/shard_map/ppermute | solution.py:37
  (46 shorter events, 5.1 us)
Async XLA Ops:
  0.6 17.2 %collective-permute-start.8 = (bf16[512,512]{1,0:T(8,128)(2,1)}, bf16[512,512]{1,0:T(8,128)(2,1)S(1)}, u32[]{:S(2)}, u32[]{:S(2)}) collective-permute-start(bf16[512,512]{1,0:T(8,128)(2,1)} %refs_1_.3), channel_id=1, source_target_pairs={{0,16},{8,24},{16,0},{24,8},{1,17},{9,25},{17,1},{25,9},{2,18},{10... | collective-permute-start | bytes 1572872 | tf_op jit(solution)/shard_map/ppermute | solution.py:37
  3.7 26.8 %collective-permute-start.7 = (bf16[512,512]{1,0:T(8,128)(2,1)}, bf16[512,512]{1,0:T(8,128)(2,1)S(1)}, u32[]{:S(2)}, u32[]{:S(2)}) collective-permute-start(bf16[512,512]{1,0:T(8,128)(2,1)} %refs_1_.3), channel_id=1, source_target_pairs={{0,8},{8,0},{16,24},{24,16},{1,9},{9,1},{17,25},{25,17},{2,10},{10... | collective-permute-start | bytes 1572872 | tf_op jit(solution)/shard_map/ppermute | solution.py:37
  5.9 9.6 %collective-permute-start = (bf16[144,512]{1,0:T(8,128)(2,1)}, bf16[144,512]{1,0:T(8,128)(2,1)S(1)}, u32[]{:S(2)}, u32[]{:S(2)}) collective-permute-start(bf16[144,512]{1,0:T(8,128)(2,1)} %get-tuple-element.25), channel_id=1, source_target_pairs={{0,2},{1,3},{2,0},{3,1},{4,6},{5,7},{6,4},{7,5},{8,10},{9,11},{10,... | collective-permute-start | bytes 442376 | tf_op jit(solution)/shard_map/ppermute | solution.py:37
  7.5 10.3 %collective-permute-start.1 = (bf16[144,512]{1,0:T(8,128)(2,1)}, bf16[144,512]{1,0:T(8,128)(2,1)S(1)}, u32[]{:S(2)}, u32[]{:S(2)}) collective-permute-start(bf16[144,512]{1,0:T(8,128)(2,1)} %get-tuple-element.26), channel_id=1, source_target_pairs={{0,4},{1,5},{2,6},{3,7},{4,0},{5,1},{6,2},{7,3},{8,12},{9,13},{10,... | collective-permute-start | bytes 442376 | tf_op jit(solution)/shard_map/ppermute | solution.py:37
  10.1 7.7 %collective-permute-start.3 = (bf16[144,512]{1,0:T(8,128)(2,1)}, bf16[144,512]{1,0:T(8,128)(2,1)S(1)}, u32[]{:S(2)}, u32[]{:S(2)}) collective-permute-start(bf16[144,512]{1,0:T(8,128)(2,1)} %get-tuple-element.24.refs_1_), channel_id=1, source_target_pairs={{0,1},{1,0},{2,3},{3,2},{4,5},{5,4},{6,7},{7,6},{8,9},{9,8},{10,11... | collective-permute-start | bytes 442376 | tf_op jit(solution)/shard_map/ppermute | solution.py:37
  17.8 2.7 %copy-start.5 = (bf16[144,512]{1,0:T(8,128)(2,1)S(1)}, bf16[144,512]{1,0:T(8,128)(2,1)}, u32[]{:S(2)}) copy-start(bf16[144,512]{1,0:T(8,128)(2,1)} %get-tuple-element.27) | copy-start | bytes 442372
  17.9 14.1 %collective-permute-start.9 = (bf16[512,512]{1,0:T(8,128)(2,1)S(1)}, bf16[512,512]{1,0:T(8,128)(2,1)S(1)}, u32[]{:S(2)}, u32[]{:S(2)}) collective-permute-start(bf16[512,512]{1,0:T(8,128)(2,1)S(1)} %shard_map.95.refs_3_), channel_id=1, source_target_pairs={{0,8},{8,0},{16,24},{24,16},{1,9},{9,1},{17,25},{25,17},{2,10},{10... | collective-permute-start | bytes 1572872 | tf_op jit(solution)/shard_map/ppermute | solution.py:37
  17.9 14.1 %copy-start = (bf16[512,512]{1,0:T(8,128)(2,1)S(1)}, bf16[512,512]{1,0:T(8,128)(2,1)}, u32[]{:S(2)}) copy-start(bf16[512,512]{1,0:T(8,128)(2,1)} %refs_1_.3) | copy-start | bytes 1572868
  18.0 14.1 %copy-start.1 = (bf16[1,128,2048]{2,1,0:T(8,128)(2,1)S(1)}, bf16[1,128,2048]{2,1,0:T(8,128)(2,1)}, u32[]{:S(2)}) copy-start(bf16[1,128,2048]{2,1,0:T(8,128)(2,1)} %param.7) | copy-start | bytes 1572868
  20.0 9.9 %collective-permute-start.14 = (bf16[2,128,512]{2,1,0:T(8,128)(2,1)}, bf16[2,128,512]{2,1,0:T(8,128)(2,1)S(1)}, u32[]{:S(2)}, u32[]{:S(2)}) collective-permute-start(bf16[2,128,512]{2,1,0:T(8,128)(2,1)} %get-tuple-element.33), channel_id=1, source_target_pairs={{0,16},{8,24},{16,0},{24,8},{1,17},{9,25},{17,1},{25,9},{2,18},{10... | collective-permute-start | bytes 786440 | tf_op jit(solution)/shard_map/ppermute | solution.py:37
  20.6 7.8 %collective-permute-start.2 = (bf16[144,512]{1,0:T(8,128)(2,1)S(1)}, bf16[144,512]{1,0:T(8,128)(2,1)S(1)}, u32[]{:S(2)}, u32[]{:S(2)}) collective-permute-start(bf16[144,512]{1,0:T(8,128)(2,1)S(1)} %copy-done.5), channel_id=1, source_target_pairs={{0,6},{1,7},{2,4},{3,5},{4,2},{5,3},{6,0},{7,1},{8,14},{9,15},{10,... | collective-permute-start | bytes 442376 | tf_op jit(solution)/shard_map/ppermute | solution.py:37
  23.3 9.4 %collective-permute-start.13 = (bf16[128,512]{1,0:T(8,128)(2,1)}, bf16[128,512]{1,0:T(8,128)(2,1)S(1)}, u32[]{:S(2)}, u32[]{:S(2)}) collective-permute-start(bf16[128,512]{1,0:T(8,128)(2,1)} %get-tuple-element.32), channel_id=1, source_target_pairs={{0,8},{8,0},{16,24},{24,16},{1,9},{9,1},{17,25},{25,17},{2,10},{10... | collective-permute-start | bytes 393224 | tf_op jit(solution)/shard_map/ppermute | solution.py:37
  28.4 6.8 %collective-permute-start.4 = (bf16[144,512]{1,0:T(8,128)(2,1)S(1)}, bf16[144,512]{1,0:T(8,128)(2,1)S(1)}, u32[]{:S(2)}, u32[]{:S(2)}) collective-permute-start(bf16[144,512]{1,0:T(8,128)(2,1)S(1)} %collective-permute-done.refs_1_.refs_5_.refs_2_), channel_id=1, source_target_pairs={{0,1},{1,0},{2,3},{3,2},{4,5},{5,4},{6,7},{7,6},{8,9},{9,8},{10,11... | collective-permute-start | bytes 442376 | tf_op jit(solution)/shard_map/ppermute | solution.py:37
  29.9 8.3 %collective-permute-start.5 = (bf16[144,512]{1,0:T(8,128)(2,1)S(1)}, bf16[144,512]{1,0:T(8,128)(2,1)S(1)}, u32[]{:S(2)}, u32[]{:S(2)}) collective-permute-start(bf16[144,512]{1,0:T(8,128)(2,1)S(1)} %collective-permute-done.1.refs_2_.refs_6_.refs_3_), channel_id=1, source_target_pairs={{0,1},{1,0},{2,3},{3,2},{4,5},{5,4},{6,7},{7,6},{8,9},{9,8},{10,11... | collective-permute-start | bytes 442376 | tf_op jit(solution)/shard_map/ppermute | solution.py:37
  30.4 10.5 %collective-permute-start.6 = (bf16[144,512]{1,0:T(8,128)(2,1)S(1)}, bf16[144,512]{1,0:T(8,128)(2,1)S(1)}, u32[]{:S(2)}, u32[]{:S(2)}) collective-permute-start(bf16[144,512]{1,0:T(8,128)(2,1)S(1)} %collective-permute-done.2.refs_7_.refs_4_), channel_id=1, source_target_pairs={{0,1},{1,0},{2,3},{3,2},{4,5},{5,4},{6,7},{7,6},{8,9},{9,8},{10,11... | collective-permute-start | bytes 442376 | tf_op jit(solution)/shard_map/ppermute | solution.py:37
  32.0 12.0 %copy-start.2 = (bf16[144,512]{1,0:T(8,128)(2,1)S(1)}, bf16[144,512]{1,0:T(8,128)(2,1)}, u32[]{:S(2)}) copy-start(bf16[144,512]{1,0:T(8,128)(2,1)} %get-tuple-element.24.refs_1_) | copy-start | bytes 442372
  32.0 8.9 %collective-permute-start.15 = (bf16[128,512]{1,0:T(8,128)(2,1)S(1)}, bf16[128,512]{1,0:T(8,128)(2,1)S(1)}, u32[]{:S(2)}, u32[]{:S(2)}) collective-permute-start(bf16[128,512]{1,0:T(8,128)(2,1)S(1)} %get-tuple-element.45), channel_id=1, source_target_pairs={{0,8},{8,0},{16,24},{24,16},{1,9},{9,1},{17,25},{25,17},{2,10},{10... | collective-permute-start | bytes 393224 | tf_op jit(solution)/shard_map/ppermute | solution.py:37
  32.6 8.3 %collective-permute-start.10 = (bf16[128,128]{1,0:T(8,128)(2,1)S(1)}, bf16[128,128]{1,0:T(8,128)(2,1)S(1)}, u32[]{:S(2)}, u32[]{:S(2)}) collective-permute-start(bf16[128,128]{1,0:T(8,128)(2,1)S(1)} %get-tuple-element.29), channel_id=1, source_target_pairs={{0,2},{1,3},{2,0},{3,1},{4,6},{5,7},{6,4},{7,5},{8,10},{9,11},{10,... | collective-permute-start | bytes 98312 | tf_op jit(solution)/shard_map/ppermute | solution.py:37
  35.2 5.7 %collective-permute-start.11 = (bf16[128,128]{1,0:T(8,128)(2,1)S(1)}, bf16[128,128]{1,0:T(8,128)(2,1)S(1)}, u32[]{:S(2)}, u32[]{:S(2)}) collective-permute-start(bf16[128,128]{1,0:T(8,128)(2,1)S(1)} %get-tuple-element.30), channel_id=1, source_target_pairs={{0,4},{1,5},{2,6},{3,7},{4,0},{5,1},{6,2},{7,3},{8,12},{9,13},{10,... | collective-permute-start | bytes 98312 | tf_op jit(solution)/shard_map/ppermute | solution.py:37
  38.2 5.7 %collective-permute-start.12 = (bf16[128,128]{1,0:T(8,128)(2,1)S(1)}, bf16[128,128]{1,0:T(8,128)(2,1)S(1)}, u32[]{:S(2)}, u32[]{:S(2)}) collective-permute-start(bf16[128,128]{1,0:T(8,128)(2,1)S(1)} %get-tuple-element.31), channel_id=1, source_target_pairs={{0,6},{1,7},{2,4},{3,5},{4,2},{5,3},{6,0},{7,1},{8,14},{9,15},{10,... | collective-permute-start | bytes 98312 | tf_op jit(solution)/shard_map/ppermute | solution.py:37
  49.7 11.8 %collective-permute-start.16 = (bf16[4,128,256]{2,1,0:T(8,128)(2,1)S(1)}, bf16[4,128,256]{2,1,0:T(8,128)(2,1)S(1)}, u32[]{:S(2)}, u32[]{:S(2)}) collective-permute-start(bf16[4,128,256]{2,1,0:T(8,128)(2,1)S(1)} %get-tuple-element.35), channel_id=1, source_target_pairs={{0,1},{1,0},{2,3},{3,2},{4,5},{5,4},{6,7},{7,6},{8,9},{9,8},{10,11... | collective-permute-start | bytes 786440 | tf_op jit(solution)/shard_map/ppermute | solution.py:37
  52.4 4.4 %collective-permute-start.20 = (bf16[128,128]{1,0:T(8,128)(2,1)S(1)}, bf16[128,128]{1,0:T(8,128)(2,1)S(1)}, u32[]{:S(2)}, u32[]{:S(2)}) collective-permute-start(bf16[128,128]{1,0:T(8,128)(2,1)S(1)} %get-tuple-element.42), channel_id=1, source_target_pairs={{0,2},{1,3},{2,0},{3,1},{4,6},{5,7},{6,4},{7,5},{8,10},{9,11},{10,... | collective-permute-start | bytes 98312 | tf_op jit(solution)/shard_map/ppermute | solution.py:37
  52.6 5.0 %collective-permute-start.21 = (bf16[128,128]{1,0:T(8,128)(2,1)S(1)}, bf16[128,128]{1,0:T(8,128)(2,1)S(1)}, u32[]{:S(2)}, u32[]{:S(2)}) collective-permute-start(bf16[128,128]{1,0:T(8,128)(2,1)S(1)} %get-tuple-element.43), channel_id=1, source_target_pairs={{0,4},{1,5},{2,6},{3,7},{4,0},{5,1},{6,2},{7,3},{8,12},{9,13},{10,... | collective-permute-start | bytes 98312 | tf_op jit(solution)/shard_map/ppermute | solution.py:37
  55.7 5.7 %collective-permute-start.22 = (bf16[128,128]{1,0:T(8,128)(2,1)S(1)}, bf16[128,128]{1,0:T(8,128)(2,1)S(1)}, u32[]{:S(2)}, u32[]{:S(2)}) collective-permute-start(bf16[128,128]{1,0:T(8,128)(2,1)S(1)} %get-tuple-element.44), channel_id=1, source_target_pairs={{0,6},{1,7},{2,4},{3,5},{4,2},{5,3},{6,0},{7,1},{8,14},{9,15},{10,... | collective-permute-start | bytes 98312 | tf_op jit(solution)/shard_map/ppermute | solution.py:37
  61.4 6.5 %copy-start.3 = (bf16[128,512]{1,0:T(8,128)(2,1)S(1)}, bf16[128,512]{1,0:T(8,128)(2,1)}, u32[]{:S(2)}) copy-start(bf16[128,512]{1,0:T(8,128)(2,1)} %get-tuple-element.40.refs_0_) | copy-start | bytes 393220
  61.5 5.0 %collective-permute-start.24 = (bf16[128,512]{1,0:T(8,128)(2,1)S(1)}, bf16[128,512]{1,0:T(8,128)(2,1)S(1)}, u32[]{:S(2)}, u32[]{:S(2)}) collective-permute-start(bf16[128,512]{1,0:T(8,128)(2,1)S(1)} %shard_map.100.refs_4_.refs_0_), channel_id=1, source_target_pairs={{0,16},{8,24},{16,0},{24,8},{1,17},{9,25},{17,1},{25,9},{2,18},{10... | collective-permute-start | bytes 393224 | tf_op jit(solution)/shard_map/ppermute | solution.py:37
  62.7 3.9 %collective-permute-start.23 = (bf16[128,512]{1,0:T(8,128)(2,1)S(1)}, bf16[128,512]{1,0:T(8,128)(2,1)S(1)}, u32[]{:S(2)}, u32[]{:S(2)}) collective-permute-start(bf16[128,512]{1,0:T(8,128)(2,1)S(1)} %shard_map.100.refs_4_.refs_0_), channel_id=1, source_target_pairs={{0,8},{8,0},{16,24},{24,16},{1,9},{9,1},{17,25},{25,17},{2,10},{10... | collective-permute-start | bytes 393224 | tf_op jit(solution)/shard_map/ppermute | solution.py:37
  66.6 1.3 %collective-permute-start.25 = (bf16[128,512]{1,0:T(8,128)(2,1)S(1)}, bf16[128,512]{1,0:T(8,128)(2,1)S(1)}, u32[]{:S(2)}, u32[]{:S(2)}) collective-permute-start(bf16[128,512]{1,0:T(8,128)(2,1)S(1)} %collective-permute-done.24.refs_6_), channel_id=1, source_target_pairs={{0,8},{8,0},{16,24},{24,16},{1,9},{9,1},{17,25},{25,17},{2,10},{10... | collective-permute-start | bytes 393224 | tf_op jit(solution)/shard_map/ppermute | solution.py:37
  69.2 24.2 %all-to-all-start = ((bf16[8,64,512]{2,1,0:T(8,128)(2,1)}), bf16[8,64,512]{2,1,0:T(8,128)(2,1)S(1)}, u32[]{:S(2)}, u32[]{:S(2)}) async-start(bf16[8,64,512]{2,1,0:T(8,128)(2,1)} %bitcast.9), calls=%async_computation | async-start | bytes 1048576 | tf_op jit(solution)/shard_map/all_to_all | solution.py:400
  72.8 11.0 %collective-permute-start.17 = (bf16[128,256]{1,0:T(8,128)(2,1)S(1)}, bf16[128,256]{1,0:T(8,128)(2,1)S(1)}, u32[]{:S(2)}, u32[]{:S(2)}) collective-permute-start(bf16[128,256]{1,0:T(8,128)(2,1)S(1)} %get-tuple-element.37), channel_id=1, source_target_pairs={{0,2},{1,3},{2,0},{3,1},{4,6},{5,7},{6,4},{7,5},{8,10},{9,11},{10,... | collective-permute-start | bytes 196616 | tf_op jit(solution)/shard_map/ppermute | solution.py:37
  74.8 17.9 %collective-permute-start.18 = (bf16[128,256]{1,0:T(8,128)(2,1)S(1)}, bf16[128,256]{1,0:T(8,128)(2,1)S(1)}, u32[]{:S(2)}, u32[]{:S(2)}) collective-permute-start(bf16[128,256]{1,0:T(8,128)(2,1)S(1)} %get-tuple-element.38), channel_id=1, source_target_pairs={{0,4},{1,5},{2,6},{3,7},{4,0},{5,1},{6,2},{7,3},{8,12},{9,13},{10,... | collective-permute-start | bytes 196616 | tf_op jit(solution)/shard_map/ppermute | solution.py:37
  77.1 15.5 %collective-permute-start.19 = (bf16[128,256]{1,0:T(8,128)(2,1)S(1)}, bf16[128,256]{1,0:T(8,128)(2,1)S(1)}, u32[]{:S(2)}, u32[]{:S(2)}) collective-permute-start(bf16[128,256]{1,0:T(8,128)(2,1)S(1)} %get-tuple-element.39), channel_id=1, source_target_pairs={{0,6},{1,7},{2,4},{3,5},{4,2},{5,3},{6,0},{7,1},{8,14},{9,15},{10,... | collective-permute-start | bytes 196616 | tf_op jit(solution)/shard_map/ppermute | solution.py:37
  (1 other events, 0.7 us)
where the time goes:
time: 94.2 us; the launch traced here: 94.1 us
  starting transfers between devices  39.6 us (42%)
  waiting for transfers between devices  38.6 us (41%)
  Pallas kernels  14.3 us (15%)
    ppermute x26, waiting for transfers between devices, swapped(): return lax.ppermute(array, axis, [(i, i ^ bits) for i in range(size)])  38.6 us
    ppermute x26, starting transfers between devices, swapped(): return lax.ppermute(array, axis, [(i, i ^ bits) for i in range(size)])  36.1 us
    pallas_call x10, Pallas kernels, call(): pl.pallas_call(body, out_shape=out_shape, in_specs=specs, out_specs=[VMEM...  14.3 us
    all_to_all x1, starting transfers between devices, shards(): lax.all_to_all(parts.reshape(devices, span // devices, columns), 'ctx', 0...  3.49 us
  transfers between devices with their start and end apart: 27, of which 12 were waited for; matrix products, arithmetic and copies ran while one was open for 0% of the time, Pallas kernels for 8%

commit v1 on v0

--- a/solution.py
+++ b/solution.py
@@ -294,7 +294,7 @@
 
 def pair_kernel(keep_ref, got_ref, *out_refs):
     for m in range(KV_HEADS):
-        out_refs[m][...] = (keep_ref[m] + got_ref[m].astype(jnp.float32)).astype(jnp.bfloat16)
+        out_refs[m][...] = (keep_ref[m] + got_ref[m].astype(jnp.float32)).astype(out_refs[m].dtype)
 
 
 def query_kernel(*rest):
@@ -314,11 +314,31 @@
         out_ref[:, pl.ds(start, span)] = matmul(grad_ref[...], w_refs[m][...], NT).astype(jnp.bfloat16)
 
 
+def weight_sums(fsdp, refs):
+    hid = jnp.concatenate([ref[...] for ref in refs[:fsdp]], axis=0)
+    grad = jnp.concatenate([ref[...] for ref in refs[fsdp:2 * fsdp]], axis=0)
+    return matmul(hid, grad, TN)
+
+
 def weight_kernel(fsdp, *rest):
-    hid_refs, grad_refs, out_ref = rest[:fsdp], rest[fsdp:2 * fsdp], rest[2 * fsdp]
-    hid = jnp.concatenate([ref[...] for ref in hid_refs], axis=0)
-    grad = jnp.concatenate([ref[...] for ref in grad_refs], axis=0)
-    out_ref[...] = matmul(hid, grad, TN).astype(jnp.bfloat16)
+    rest[2 * fsdp][...] = weight_sums(fsdp, rest).astype(jnp.bfloat16)
+
+
+def sides_kernel(fsdp, *rest):
+    keep_ref, send_ref, parts = rest[2 * fsdp:]
+    head, side = head_side()
+    parts[...] = weight_sums(fsdp, rest).reshape(parts.shape)
+    for m in range(KV_HEADS):
+        to = 2 * jnp.bitwise_xor(head, m)
+        keep_ref[m] = parts[to + side]
+        send_ref[m] = parts[to + 1 - side].astype(jnp.bfloat16)
+
+
+def own_total_kernel(own_ref, *rest):
+    total = own_ref[...]
+    for ref in rest[:-1]:
+        total = total + ref[...].astype(jnp.float32)
+    rest[-1][...] = total
 
 
 def total_kernel(part_ref, out_ref):
@@ -360,17 +380,17 @@
         (queries[0], grad_out[0], attn_out[0], log_sums[0]), hbm=4)
     qd = along_heads(qd)
     qd = qd + [swapped(one, "ctx", 1) for one in qd]
-    w_far = held(swapped(w_kv, "fsdp", far), (qd[1], qd[2], qd[KV_HEADS]))
-    w_parts = over_fsdp([w_kv] * far + [w_far] * (fsdp - far), far // 2)
-
-    kv = call(
-        functools.partial(project_kernel, fsdp), [sds(block)] * KV_HEADS,
-        [pltpu.VMEM((KV_HEADS,) + block, jnp.bfloat16)], (inputs, *w_parts), after=(*qd[1:KV_HEADS], qd[KV_HEADS]))
-    kv = along_heads(kv)
-
     *hid, hid_far = call(
         functools.partial(hidden_kernel, fsdp), [sds((rows, span))] * far + [sds((fsdp - far, rows, span))],
         [pltpu.SemaphoreType.DMA((fsdp,))], (inputs,), hbm=1)
+    w_far = held(swapped(w_kv, "fsdp", far), (*qd[1:KV_HEADS + 3], hid_far))
+    w_parts = over_fsdp([w_kv] * far + [w_far] * (fsdp - far), far // 2)
+
+    kv = call(
+        functools.partial(project_kernel, fsdp), [sds(block)] * KV_HEADS,
+        [pltpu.VMEM((KV_HEADS,) + block, jnp.bfloat16)], (inputs, *w_parts))
+    kv = along_heads(kv)
+
     hid_far = swapped(hid_far, "fsdp", far)
     hid = over_fsdp(hid + [hid_far[m] for m in range(fsdp - far)], far // 2)
 
@@ -381,7 +401,7 @@
             [pltpu.VMEM((TEAM,) + wide, jnp.bfloat16)] * 2 + [pltpu.VMEM((TEAM, 2 * GROUPS, rows), f32)]
             + [pltpu.VMEM((TEAM, 2 * rows, PAIR), jnp.bfloat16)] * 2
             + [pltpu.VMEM((TEAM,) + wide, f32), pltpu.VMEM((TEAM,) + block, f32)],
-            (block_order, *qd, *kv), smem=1, after=hid[1:])
+            (block_order, *qd, *kv), smem=1, after=(hid_far,))
     else:
         alike = [[t * TEAM + i for t in range(teams)] for i in range(TEAM)]
         kv = lax.all_gather(jnp.stack(kv), "ctx", axis_index_groups=alike, axis=0, tiled=True)
@@ -391,18 +411,31 @@
         dkv = lax.psum_scatter(dkv, "ctx", axis_index_groups=alike, scatter_dimension=0, tiled=True)
         dkv = [dkv[m].astype(jnp.bfloat16) for m in range(KV_HEADS)]
 
-    give = swapped(give, "ctx", 1)
+    dkv = along_heads(dkv)
+    give = swapped(held(give, dkv[1:]), "ctx", 1)
     (kv_grad,) = call(
         owner_kernel, [sds((rows, columns))], [pltpu.VMEM((KV_HEADS,) + block, jnp.bfloat16)],
-        along_heads(dkv), after=(give,))
+        dkv)
     grads = over_fsdp([kv_grad] * fsdp, far)
-    (parts,) = call(functools.partial(weight_kernel, fsdp), [sds((span, columns))], [], (*hid, *grads))
-    sums = lax.all_to_all(parts.reshape(devices, span // devices, columns), "ctx", 0, 0, tiled=True)
-
-    dq = call(pair_kernel, [sds(wide)] * KV_HEADS, [], (keep, give))
-    (query_grads,) = call(query_kernel, [sds((rows, Q_HEADS * HEAD_DIM))], [], along_heads(dq), after=(parts,))
-    (input_grads,) = call(functools.partial(input_kernel, fsdp), [sds((rows, model))], [], (kv_grad, *w_parts), after=(parts,))
-    (weight_grads,) = call(total_kernel, [sds((span // devices, columns), f32)], [], (sums,))
+    if teams == 1:
+        share = (span // devices, columns)
+        own_sums, send_sums = call(
+            functools.partial(sides_kernel, fsdp), [sds((KV_HEADS,) + share, f32), sds((KV_HEADS,) + share)],
+            [pltpu.VMEM((devices,) + share, f32)], (*hid, *grads))
+        formed = (own_sums,)
+        dq = along_heads(call(pair_kernel, [sds(wide)] * KV_HEADS, [], (keep, give), after=formed))
+        sums = call(
+            pair_kernel, [sds(share, f32)] + [sds(share)] * (KV_HEADS - 1), [],
+            (own_sums, swapped(send_sums, "ctx", 1)), after=dq[1:])
+        (weight_grads,) = call(own_total_kernel, [sds(share, f32)], [], along_heads(sums))
+    else:
+        formed = call(functools.partial(weight_kernel, fsdp), [sds((span, columns))], [], (*hid, *grads))
+        dq = along_heads(call(pair_kernel, [sds(wide)] * KV_HEADS, [], (keep, give), after=formed))
+        sums = lax.all_to_all(formed[0].reshape(devices, span // devices, columns), "ctx", 0, 0, tiled=True)
+        (weight_grads,) = call(total_kernel, [sds((span // devices, columns), f32)], [], (sums,))
+    (query_grads,) = call(query_kernel, [sds((rows, Q_HEADS * HEAD_DIM))], [], dq, after=formed)
+    (input_grads,) = call(
+        functools.partial(input_kernel, fsdp), [sds((rows, model))], [], (kv_grad, *w_parts), after=formed)
     return query_grads[None], input_grads[None], weight_grads
 
 

time: 94.2 us -> 85.4 us (0.907)
  waiting for transfers between devices: 38.6 us -> 32.8 us
  starting transfers between devices: 39.6 us -> 36.2 us
    ppermute x26 -> x30, waiting for transfers between devices: 38.6 us -> 32.8 us  [swapped(): return lax.ppermute(array, axis, [(i, i ^ bits) for i in range(size)])]
    all_to_all x1 -> x0, starting transfers between devices: 3.49 us -> none  [shards(): lax.all_to_all(parts.reshape(devices, span // devices, columns), 'ctx', 0...]
    pallas_call x10 -> x11, Pallas kernels: 14.3 us -> 14.2 us  [call(): pl.pallas_call(body, out_shape=out_shape, in_specs=specs, out_specs=[VMEM...]
    ppermute x26 -> x30, starting transfers between devices: 36.1 us -> 36.2 us  [swapped(): return lax.ppermute(array, axis, [(i, i ^ bits) for i in range(size)])]
  transfers between devices with their start and end apart: 27 -> 30, of which waited for: 12 -> 12; matrix products, arithmetic and copies ran while one was open for 0% -> 0% of each run, Pallas kernels for 8% -> 9%
where the time goes in v1:
time: 85.4 us; the launch traced here: 85 us
  starting transfers between devices  36.2 us (42%)
  waiting for transfers between devices  32.8 us (38%)
  Pallas kernels  14.2 us (17%)
  local copies, waits for them, and re-layouts  0.99 us (1%)
    ppermute x30, starting transfers between devices, swapped(): return lax.ppermute(array, axis, [(i, i ^ bits) for i in range(size)])  36.2 us
    ppermute x30, waiting for transfers between devices, swapped(): return lax.ppermute(array, axis, [(i, i ^ bits) for i in range(size)])  32.8 us
    pallas_call x11, Pallas kernels, call(): pl.pallas_call(body, out_shape=out_shape, in_specs=specs, out_specs=[VMEM...  14.2 us
  transfers between devices with their start and end apart: 30, of which 12 were waited for; matrix products, arithmetic and copies ran while one was open for 0% of the time, Pallas kernels for 9%

profile of v1, /device:TPU:0, one launch (start us, length us, event | category | flops | bytes accessed | tf_op | source)
XLA Modules:
  0.0 85.0 jit_solution(4434284372663860805)
XLA Ops:
  0.6 3.0 %collective-permute-start.8 = (bf16[512,512]{1,0:T(8,128)(2,1)}, bf16[512,512]{1,0:T(8,128)(2,1)S(1)}, u32[]{:S(2)}, u32[]{:S(2)}) collective-permute-start(bf16[512,512]{1,0:T(8,128)(2,1)} %refs_1_.3), channel_id=1, source_target_pairs={{0,16},{8,24},{16,0},{24,8},{1,17},{9,25},{17,1},{25,9},{2,18},{10... | collective-permute-start | bytes 1572872 | tf_op jit(solution)/shard_map/ppermute | solution.py:37
  3.7 2.3 %shard_map.94 = (bf16[144,512]{1,0:T(8,128)(2,1)}, bf16[144,512]{1,0:T(8,128)(2,1)}, bf16[144,512]{1,0:T(8,128)(2,1)}, bf16[144,512]{1,0:T(8,128)(2,1)}) custom-call(bf16[128,1024]{1,0:T(8,128)(2,1)} %bitcast.14, bf16[128,1024]{1,0:T(8,128)(2,1)} %bitcast.15, bf16[128,1024]{1,0:T(8,128)(2,1)} %bitcast.16, f32[16,128]{1,0:T(8,128)} %bitcast.18), custom_call_target="tpu_custom_call" | custom-call | tf_op jit(solution)/shard_map/pallas_call | solution.py:48
  6.0 1.6 %collective-permute-start = (bf16[144,512]{1,0:T(8,128)(2,1)}, bf16[144,512]{1,0:T(8,128)(2,1)S(1)}, u32[]{:S(2)}, u32[]{:S(2)}) collective-permute-start(bf16[144,512]{1,0:T(8,128)(2,1)} %get-tuple-element.31), channel_id=1, source_target_pairs={{0,2},{1,3},{2,0},{3,1},{4,6},{5,7},{6,4},{7,5},{8,10},{9,11},{10,... | collective-permute-start | bytes 442376 | tf_op jit(solution)/shard_map/ppermute | solution.py:37
  7.6 2.6 %collective-permute-start.1 = (bf16[144,512]{1,0:T(8,128)(2,1)}, bf16[144,512]{1,0:T(8,128)(2,1)S(1)}, u32[]{:S(2)}, u32[]{:S(2)}) collective-permute-start(bf16[144,512]{1,0:T(8,128)(2,1)} %get-tuple-element.32), channel_id=1, source_target_pairs={{0,4},{1,5},{2,6},{3,7},{4,0},{5,1},{6,2},{7,3},{8,12},{9,13},{10,... | collective-permute-start | bytes 442376 | tf_op jit(solution)/shard_map/ppermute | solution.py:37
  10.4 1.5 %collective-permute-start.3 = (bf16[144,512]{1,0:T(8,128)(2,1)}, bf16[144,512]{1,0:T(8,128)(2,1)S(1)}, u32[]{:S(2)}, u32[]{:S(2)}) collective-permute-start(bf16[144,512]{1,0:T(8,128)(2,1)} %get-tuple-element.30.refs_1_), channel_id=1, source_target_pairs={{0,1},{1,0},{2,3},{3,2},{4,5},{5,4},{6,7},{7,6},{8,9},{9,8},{10,11... | collective-permute-start | bytes 442376 | tf_op jit(solution)/shard_map/ppermute | solution.py:37
  11.9 1.5 %collective-permute-done.refs_1_.refs_2_ = bf16[144,512]{1,0:T(8,128)(2,1)S(1)} collective-permute-done((bf16[144,512]{1,0:T(8,128)(2,1)}, bf16[144,512]{1,0:T(8,128)(2,1)S(1)}, u32[]{:S(2)}, u32[]{:S(2)}) %collective-permute-start) | collective-permute-done | bytes 147488 | tf_op jit(solution)/shard_map/ppermute | solution.py:37
  13.4 1.5 %collective-permute-start.4 = (bf16[144,512]{1,0:T(8,128)(2,1)S(1)}, bf16[144,512]{1,0:T(8,128)(2,1)S(1)}, u32[]{:S(2)}, u32[]{:S(2)}) collective-permute-start(bf16[144,512]{1,0:T(8,128)(2,1)S(1)} %collective-permute-done.refs_1_.refs_2_), channel_id=1, source_target_pairs={{0,1},{1,0},{2,3},{3,2},{4,5},{5,4},{6,7},{7,6},{8,9},{9,8},{10,11... | collective-permute-start | bytes 442376 | tf_op jit(solution)/shard_map/ppermute | solution.py:37
  14.9 6.8 %collective-permute-done.1.refs_2_.refs_3_ = bf16[144,512]{1,0:T(8,128)(2,1)S(1)} collective-permute-done((bf16[144,512]{1,0:T(8,128)(2,1)}, bf16[144,512]{1,0:T(8,128)(2,1)S(1)}, u32[]{:S(2)}, u32[]{:S(2)}) %collective-permute-start.1) | collective-permute-done | bytes 147488 | tf_op jit(solution)/shard_map/ppermute | solution.py:37
  21.7 1.5 %collective-permute-start.5 = (bf16[144,512]{1,0:T(8,128)(2,1)S(1)}, bf16[144,512]{1,0:T(8,128)(2,1)S(1)}, u32[]{:S(2)}, u32[]{:S(2)}) collective-permute-start(bf16[144,512]{1,0:T(8,128)(2,1)S(1)} %collective-permute-done.1.refs_2_.refs_3_), channel_id=1, source_target_pairs={{0,1},{1,0},{2,3},{3,2},{4,5},{5,4},{6,7},{7,6},{8,9},{9,8},{10,11... | collective-permute-start | bytes 442376 | tf_op jit(solution)/shard_map/ppermute | solution.py:37
  23.2 1.9 %shard_map.95 = (bf16[128,512]{1,0:T(8,128)(2,1)}, bf16[128,512]{1,0:T(8,128)(2,1)}, bf16[2,128,512]{2,1,0:T(8,128)(2,1)}) custom-call(bf16[128,2048]{1,0:T(8,128)(2,1)} %bitcast.11), custom_call_target="tpu_custom_call" | custom-call | tf_op jit(solution)/shard_map/pallas_call | solution.py:48
  25.2 1.6 %collective-permute-done.5.refs_6_.refs_7_ = bf16[144,512]{1,0:T(8,128)(2,1)S(1)} collective-permute-done((bf16[144,512]{1,0:T(8,128)(2,1)S(1)}, bf16[144,512]{1,0:T(8,128)(2,1)S(1)}, u32[]{:S(2)}, u32[]{:S(2)}) %collective-permute-start.5) | collective-permute-done | bytes 147488 | tf_op jit(solution)/shard_map/ppermute | solution.py:37
  28.4 1.5 %collective-permute-start.6 = (bf16[144,512]{1,0:T(8,128)(2,1)S(1)}, bf16[144,512]{1,0:T(8,128)(2,1)S(1)}, u32[]{:S(2)}, u32[]{:S(2)}) collective-permute-start(bf16[144,512]{1,0:T(8,128)(2,1)S(1)} %collective-permute-done.2.refs_3_.refs_4_), channel_id=1, source_target_pairs={{0,1},{1,0},{2,3},{3,2},{4,5},{5,4},{6,7},{7,6},{8,9},{9,8},{10,11... | collective-permute-start | bytes 442376 | tf_op jit(solution)/shard_map/ppermute | solution.py:37
  30.5 2.8 %collective-permute-start.11 = (bf16[128,128]{1,0:T(8,128)(2,1)S(1)}, bf16[128,128]{1,0:T(8,128)(2,1)S(1)}, u32[]{:S(2)}, u32[]{:S(2)}) collective-permute-start(bf16[128,128]{1,0:T(8,128)(2,1)S(1)} %get-tuple-element.37), channel_id=1, source_target_pairs={{0,4},{1,5},{2,6},{3,7},{4,0},{5,1},{6,2},{7,3},{8,12},{9,13},{10,... | collective-permute-start | bytes 98312 | tf_op jit(solution)/shard_map/ppermute | solution.py:37
  33.3 1.6 %collective-permute-start.12 = (bf16[128,128]{1,0:T(8,128)(2,1)S(1)}, bf16[128,128]{1,0:T(8,128)(2,1)S(1)}, u32[]{:S(2)}, u32[]{:S(2)}) collective-permute-start(bf16[128,128]{1,0:T(8,128)(2,1)S(1)} %get-tuple-element.38), channel_id=1, source_target_pairs={{0,6},{1,7},{2,4},{3,5},{4,2},{5,3},{6,0},{7,1},{8,14},{9,15},{10,... | collective-permute-start | bytes 98312 | tf_op jit(solution)/shard_map/ppermute | solution.py:37
  34.9 1.6 %collective-permute-done.13.refs_13_ = bf16[2,128,512]{2,1,0:T(8,128)(2,1)S(1)} collective-permute-done((bf16[2,128,512]{2,1,0:T(8,128)(2,1)S(1)}, bf16[2,128,512]{2,1,0:T(8,128)(2,1)S(1)}, u32[]{:S(2)}, u32[]{:S(2)}) %collective-permute-start.13) | collective-permute-done | bytes 262176 | tf_op jit(solution)/shard_map/ppermute | solution.py:37
  36.5 2.5 %collective-permute-done.12.refs_12_ = bf16[128,128]{1,0:T(8,128)(2,1)S(1)} collective-permute-done((bf16[128,128]{1,0:T(8,128)(2,1)S(1)}, bf16[128,128]{1,0:T(8,128)(2,1)S(1)}, u32[]{:S(2)}, u32[]{:S(2)}) %collective-permute-start.12) | collective-permute-done | bytes 32800 | tf_op jit(solution)/shard_map/ppermute | solution.py:37
  39.0 5.7 %shard_map.98 = (bf16[128,128]{1,0:T(8,128)(2,1)S(1)}, bf16[128,128]{1,0:T(8,128)(2,1)S(1)}, bf16[128,128]{1,0:T(8,128)(2,1)S(1)}, bf16[128,128]{1,0:T(8,128)(2,...) custom-call(s32[1,8]{1,0:T(1,128)S(1)} %copy-done.5, bf16[144,512]{1,0:T(8,128)(2,1)S(1)} %copy-done.3, ...), custom_call_target="tpu_custom_call" | custom-call | tf_op jit(solution)/shard_map/pallas_call | solution.py:48
  44.8 2.1 %collective-permute-start.15 = (bf16[128,128]{1,0:T(8,128)(2,1)S(1)}, bf16[128,128]{1,0:T(8,128)(2,1)S(1)}, u32[]{:S(2)}, u32[]{:S(2)}) collective-permute-start(bf16[128,128]{1,0:T(8,128)(2,1)S(1)} %get-tuple-element.42), channel_id=1, source_target_pairs={{0,4},{1,5},{2,6},{3,7},{4,0},{5,1},{6,2},{7,3},{8,12},{9,13},{10,... | collective-permute-start | bytes 98312 | tf_op jit(solution)/shard_map/ppermute | solution.py:37
  46.9 2.3 %collective-permute-start.16 = (bf16[128,128]{1,0:T(8,128)(2,1)S(1)}, bf16[128,128]{1,0:T(8,128)(2,1)S(1)}, u32[]{:S(2)}, u32[]{:S(2)}) collective-permute-start(bf16[128,128]{1,0:T(8,128)(2,1)S(1)} %get-tuple-element.43), channel_id=1, source_target_pairs={{0,6},{1,7},{2,4},{3,5},{4,2},{5,3},{6,0},{7,1},{8,14},{9,15},{10,... | collective-permute-start | bytes 98312 | tf_op jit(solution)/shard_map/ppermute | solution.py:37
  49.7 2.9 %collective-permute-done.16.refs_3_ = bf16[128,128]{1,0:T(8,128)(2,1)S(1)} collective-permute-done((bf16[128,128]{1,0:T(8,128)(2,1)S(1)}, bf16[128,128]{1,0:T(8,128)(2,1)S(1)}, u32[]{:S(2)}, u32[]{:S(2)}) %collective-permute-start.16) | collective-permute-done | bytes 32800 | tf_op jit(solution)/shard_map/ppermute | solution.py:37
  54.1 3.7 %collective-permute-done.21.refs_6_ = bf16[128,512]{1,0:T(8,128)(2,1)S(1)} collective-permute-done((bf16[128,512]{1,0:T(8,128)(2,1)S(1)}, bf16[128,512]{1,0:T(8,128)(2,1)S(1)}, u32[]{:S(2)}, u32[]{:S(2)}) %collective-permute-start.21) | collective-permute-done | bytes 131104 | tf_op jit(solution)/shard_map/ppermute | solution.py:37
  57.8 1.6 %collective-permute-start.17 = (bf16[4,128,256]{2,1,0:T(8,128)(2,1)S(1)}, bf16[4,128,256]{2,1,0:T(8,128)(2,1)S(1)}, u32[]{:S(2)}, u32[]{:S(2)}) collective-permute-start(bf16[4,128,256]{2,1,0:T(8,128)(2,1)S(1)} %shard_map.99), channel_id=1, source_target_pairs={{0,1},{1,0},{2,3},{3,2},{4,5},{5,4},{6,7},{7,6},{8,9},{9,8},{10,11... | collective-permute-start | bytes 786440 | tf_op jit(solution)/shard_map/ppermute | solution.py:37
  60.0 1.4 %collective-permute-start.26 = (bf16[4,64,512]{2,1,0:T(8,128)(2,1)S(1)}, bf16[4,64,512]{2,1,0:T(8,128)(2,1)S(1)}, u32[]{:S(2)}, u32[]{:S(2)}) collective-permute-start(bf16[4,64,512]{2,1,0:T(8,128)(2,1)S(1)} %get-tuple-element.52), channel_id=1, source_target_pairs={{0,1},{1,0},{2,3},{3,2},{4,5},{5,4},{6,7},{7,6},{8,9},{9,8},{10,11... | collective-permute-start | bytes 786440 | tf_op jit(solution)/shard_map/ppermute | solution.py:37
  61.4 5.5 %collective-permute-done.17.refs_1_ = bf16[4,128,256]{2,1,0:T(8,128)(2,1)S(1)} collective-permute-done((bf16[4,128,256]{2,1,0:T(8,128)(2,1)S(1)}, bf16[4,128,256]{2,1,0:T(8,128)(2,1)S(1)}, u32[]{:S(2)}, u32[]{:S(2)}) %collective-permute-start.17) | collective-permute-done | bytes 262176 | tf_op jit(solution)/shard_map/ppermute | solution.py:37
  67.0 2.8 %collective-permute-start.24 = (bf16[128,256]{1,0:T(8,128)(2,1)S(1)}, bf16[128,256]{1,0:T(8,128)(2,1)S(1)}, u32[]{:S(2)}, u32[]{:S(2)}) collective-permute-start(bf16[128,256]{1,0:T(8,128)(2,1)S(1)} %get-tuple-element.50), channel_id=1, source_target_pairs={{0,4},{1,5},{2,6},{3,7},{4,0},{5,1},{6,2},{7,3},{8,12},{9,13},{10,... | collective-permute-start | bytes 196616 | tf_op jit(solution)/shard_map/ppermute | solution.py:37
  69.9 1.6 %collective-permute-start.25 = (bf16[128,256]{1,0:T(8,128)(2,1)S(1)}, bf16[128,256]{1,0:T(8,128)(2,1)S(1)}, u32[]{:S(2)}, u32[]{:S(2)}) collective-permute-start(bf16[128,256]{1,0:T(8,128)(2,1)S(1)} %get-tuple-element.51), channel_id=1, source_target_pairs={{0,6},{1,7},{2,4},{3,5},{4,2},{5,3},{6,0},{7,1},{8,14},{9,15},{10,... | collective-permute-start | bytes 196616 | tf_op jit(solution)/shard_map/ppermute | solution.py:37
  71.4 3.1 %collective-permute-done.24.refs_2_.refs_3_ = bf16[128,256]{1,0:T(8,128)(2,1)S(1)} collective-permute-done((bf16[128,256]{1,0:T(8,128)(2,1)S(1)}, bf16[128,256]{1,0:T(8,128)(2,1)S(1)}, u32[]{:S(2)}, u32[]{:S(2)}) %collective-permute-start.24) | collective-permute-done | bytes 65568 | tf_op jit(solution)/shard_map/ppermute | solution.py:37
  74.5 1.4 %collective-permute-done.25.refs_3_.refs_4_ = bf16[128,256]{1,0:T(8,128)(2,1)S(1)} collective-permute-done((bf16[128,256]{1,0:T(8,128)(2,1)S(1)}, bf16[128,256]{1,0:T(8,128)(2,1)S(1)}, u32[]{:S(2)}, u32[]{:S(2)}) %collective-permute-start.25) | collective-permute-done | bytes 65568 | tf_op jit(solution)/shard_map/ppermute | solution.py:37
  76.1 2.2 %collective-permute-start.28 = (bf16[64,512]{1,0:T(8,128)(2,1)S(1)}, bf16[64,512]{1,0:T(8,128)(2,1)S(1)}, u32[]{:S(2)}, u32[]{:S(2)}) collective-permute-start(bf16[64,512]{1,0:T(8,128)(2,1)S(1)} %get-tuple-element.55), channel_id=1, source_target_pairs={{0,4},{1,5},{2,6},{3,7},{4,0},{5,1},{6,2},{7,3},{8,12},{9,13},{10,... | collective-permute-start | bytes 196616 | tf_op jit(solution)/shard_map/ppermute | solution.py:37
  78.3 2.2 %collective-permute-start.29 = (bf16[64,512]{1,0:T(8,128)(2,1)S(1)}, bf16[64,512]{1,0:T(8,128)(2,1)S(1)}, u32[]{:S(2)}, u32[]{:S(2)}) collective-permute-start(bf16[64,512]{1,0:T(8,128)(2,1)S(1)} %get-tuple-element.56), channel_id=1, source_target_pairs={{0,6},{1,7},{2,4},{3,5},{4,2},{5,3},{6,0},{7,1},{8,14},{9,15},{10,... | collective-permute-start | bytes 196616 | tf_op jit(solution)/shard_map/ppermute | solution.py:37
  80.5 1.6 %shard_map.104 = bf16[128,2048]{1,0:T(8,128)(2,1)} custom-call(bf16[128,512]{1,0:T(8,128)(2,1)S(1)} %shard_map.100.refs_4_.refs_0_, bf16[512,512]{1,0:T(8,128)(2,1)S(1)} %copy-done, bf16[512,512]{1,0:T(8,128)(2,1)S(1)} %collective-permute-done.7.refs_2_, bf16[512,512]{1,0:T(8,128)(2,1)S(1)} %shard_map.96.refs_3_, ...), custom_call_target="tpu_custom_call" | custom-call | tf_op jit(solution)/shard_map/pallas_call | solution.py:48
  82.8 1.5 %collective-permute-done.29.refs_3_ = bf16[64,512]{1,0:T(8,128)(2,1)S(1)} collective-permute-done((bf16[64,512]{1,0:T(8,128)(2,1)S(1)}, bf16[64,512]{1,0:T(8,128)(2,1)S(1)}, u32[]{:S(2)}, u32[]{:S(2)}) %collective-permute-start.29) | collective-permute-done | bytes 65568 | tf_op jit(solution)/shard_map/ppermute | solution.py:37
  (56 shorter events, 6.7 us)
Async XLA Ops:
  0.6 26.2 %collective-permute-start.8 = (bf16[512,512]{1,0:T(8,128)(2,1)}, bf16[512,512]{1,0:T(8,128)(2,1)S(1)}, u32[]{:S(2)}, u32[]{:S(2)}) collective-permute-start(bf16[512,512]{1,0:T(8,128)(2,1)} %refs_1_.3), channel_id=1, source_target_pairs={{0,16},{8,24},{16,0},{24,8},{1,17},{9,25},{17,1},{25,9},{2,18},{10... | collective-permute-start | bytes 1572872 | tf_op jit(solution)/shard_map/ppermute | solution.py:37
  3.7 21.4 %copy-start = (bf16[512,512]{1,0:T(8,128)(2,1)S(1)}, bf16[512,512]{1,0:T(8,128)(2,1)}, u32[]{:S(2)}) copy-start(bf16[512,512]{1,0:T(8,128)(2,1)} %refs_1_.3) | copy-start | bytes 1572868
  6.0 7.4 %collective-permute-start = (bf16[144,512]{1,0:T(8,128)(2,1)}, bf16[144,512]{1,0:T(8,128)(2,1)S(1)}, u32[]{:S(2)}, u32[]{:S(2)}) collective-permute-start(bf16[144,512]{1,0:T(8,128)(2,1)} %get-tuple-element.31), channel_id=1, source_target_pairs={{0,2},{1,3},{2,0},{3,1},{4,6},{5,7},{6,4},{7,5},{8,10},{9,11},{10,... | collective-permute-start | bytes 442376 | tf_op jit(solution)/shard_map/ppermute | solution.py:37
  7.6 14.1 %collective-permute-start.1 = (bf16[144,512]{1,0:T(8,128)(2,1)}, bf16[144,512]{1,0:T(8,128)(2,1)S(1)}, u32[]{:S(2)}, u32[]{:S(2)}) collective-permute-start(bf16[144,512]{1,0:T(8,128)(2,1)} %get-tuple-element.32), channel_id=1, source_target_pairs={{0,4},{1,5},{2,6},{3,7},{4,0},{5,1},{6,2},{7,3},{8,12},{9,13},{10,... | collective-permute-start | bytes 442376 | tf_op jit(solution)/shard_map/ppermute | solution.py:37
  10.2 14.9 %collective-permute-start.2 = (bf16[144,512]{1,0:T(8,128)(2,1)}, bf16[144,512]{1,0:T(8,128)(2,1)S(1)}, u32[]{:S(2)}, u32[]{:S(2)}) collective-permute-start(bf16[144,512]{1,0:T(8,128)(2,1)} %get-tuple-element.33), channel_id=1, source_target_pairs={{0,6},{1,7},{2,4},{3,5},{4,2},{5,3},{6,0},{7,1},{8,14},{9,15},{10,... | collective-permute-start | bytes 442376 | tf_op jit(solution)/shard_map/ppermute | solution.py:37
  10.4 14.8 %collective-permute-start.3 = (bf16[144,512]{1,0:T(8,128)(2,1)}, bf16[144,512]{1,0:T(8,128)(2,1)S(1)}, u32[]{:S(2)}, u32[]{:S(2)}) collective-permute-start(bf16[144,512]{1,0:T(8,128)(2,1)} %get-tuple-element.30.refs_1_), channel_id=1, source_target_pairs={{0,1},{1,0},{2,3},{3,2},{4,5},{5,4},{6,7},{7,6},{8,9},{9,8},{10,11... | collective-permute-start | bytes 442376 | tf_op jit(solution)/shard_map/ppermute | solution.py:37
  13.4 11.9 %collective-permute-start.4 = (bf16[144,512]{1,0:T(8,128)(2,1)S(1)}, bf16[144,512]{1,0:T(8,128)(2,1)S(1)}, u32[]{:S(2)}, u32[]{:S(2)}) collective-permute-start(bf16[144,512]{1,0:T(8,128)(2,1)S(1)} %collective-permute-done.refs_1_.refs_2_), channel_id=1, source_target_pairs={{0,1},{1,0},{2,3},{3,2},{4,5},{5,4},{6,7},{7,6},{8,9},{9,8},{10,11... | collective-permute-start | bytes 442376 | tf_op jit(solution)/shard_map/ppermute | solution.py:37
  21.7 5.1 %collective-permute-start.5 = (bf16[144,512]{1,0:T(8,128)(2,1)S(1)}, bf16[144,512]{1,0:T(8,128)(2,1)S(1)}, u32[]{:S(2)}, u32[]{:S(2)}) collective-permute-start(bf16[144,512]{1,0:T(8,128)(2,1)S(1)} %collective-permute-done.1.refs_2_.refs_3_), channel_id=1, source_target_pairs={{0,1},{1,0},{2,3},{3,2},{4,5},{5,4},{6,7},{7,6},{8,9},{9,8},{10,11... | collective-permute-start | bytes 442376 | tf_op jit(solution)/shard_map/ppermute | solution.py:37
  25.1 4.7 %collective-permute-start.7 = (bf16[512,512]{1,0:T(8,128)(2,1)S(1)}, bf16[512,512]{1,0:T(8,128)(2,1)S(1)}, u32[]{:S(2)}, u32[]{:S(2)}) collective-permute-start(bf16[512,512]{1,0:T(8,128)(2,1)S(1)} %copy-done), channel_id=1, source_target_pairs={{0,8},{8,0},{16,24},{24,16},{1,9},{9,1},{17,25},{25,17},{2,10},{10... | collective-permute-start | bytes 1572872 | tf_op jit(solution)/shard_map/ppermute | solution.py:37
  27.8 11.2 %copy-start.3 = (bf16[144,512]{1,0:T(8,128)(2,1)S(1)}, bf16[144,512]{1,0:T(8,128)(2,1)}, u32[]{:S(2)}) copy-start(bf16[144,512]{1,0:T(8,128)(2,1)} %get-tuple-element.30.refs_1_) | copy-start | bytes 442372
  27.8 2.1 %collective-permute-start.9 = (bf16[512,512]{1,0:T(8,128)(2,1)S(1)}, bf16[512,512]{1,0:T(8,128)(2,1)S(1)}, u32[]{:S(2)}, u32[]{:S(2)}) collective-permute-start(bf16[512,512]{1,0:T(8,128)(2,1)S(1)} %shard_map.96.refs_3_), channel_id=1, source_target_pairs={{0,8},{8,0},{16,24},{24,16},{1,9},{9,1},{17,25},{25,17},{2,10},{10... | collective-permute-start | bytes 1572872 | tf_op jit(solution)/shard_map/ppermute | solution.py:37
  27.8 8.7 %collective-permute-start.13 = (bf16[2,128,512]{2,1,0:T(8,128)(2,1)S(1)}, bf16[2,128,512]{2,1,0:T(8,128)(2,1)S(1)}, u32[]{:S(2)}, u32[]{:S(2)}) collective-permute-start(bf16[2,128,512]{2,1,0:T(8,128)(2,1)S(1)} %copy-done.2), channel_id=1, source_target_pairs={{0,16},{8,24},{16,0},{24,8},{1,17},{9,25},{17,1},{25,9},{2,18},{10... | collective-permute-start | bytes 786440 | tf_op jit(solution)/shard_map/ppermute | solution.py:37
  28.4 8.1 %collective-permute-start.6 = (bf16[144,512]{1,0:T(8,128)(2,1)S(1)}, bf16[144,512]{1,0:T(8,128)(2,1)S(1)}, u32[]{:S(2)}, u32[]{:S(2)}) collective-permute-start(bf16[144,512]{1,0:T(8,128)(2,1)S(1)} %collective-permute-done.2.refs_3_.refs_4_), channel_id=1, source_target_pairs={{0,1},{1,0},{2,3},{3,2},{4,5},{5,4},{6,7},{7,6},{8,9},{9,8},{10,11... | collective-permute-start | bytes 442376 | tf_op jit(solution)/shard_map/ppermute | solution.py:37
  30.4 6.1 %collective-permute-start.10 = (bf16[128,128]{1,0:T(8,128)(2,1)S(1)}, bf16[128,128]{1,0:T(8,128)(2,1)S(1)}, u32[]{:S(2)}, u32[]{:S(2)}) collective-permute-start(bf16[128,128]{1,0:T(8,128)(2,1)S(1)} %get-tuple-element.36), channel_id=1, source_target_pairs={{0,2},{1,3},{2,0},{3,1},{4,6},{5,7},{6,4},{7,5},{8,10},{9,11},{10,... | collective-permute-start | bytes 98312 | tf_op jit(solution)/shard_map/ppermute | solution.py:37
  30.5 6.0 %collective-permute-start.11 = (bf16[128,128]{1,0:T(8,128)(2,1)S(1)}, bf16[128,128]{1,0:T(8,128)(2,1)S(1)}, u32[]{:S(2)}, u32[]{:S(2)}) collective-permute-start(bf16[128,128]{1,0:T(8,128)(2,1)S(1)} %get-tuple-element.37), channel_id=1, source_target_pairs={{0,4},{1,5},{2,6},{3,7},{4,0},{5,1},{6,2},{7,3},{8,12},{9,13},{10,... | collective-permute-start | bytes 98312 | tf_op jit(solution)/shard_map/ppermute | solution.py:37
  33.3 5.7 %collective-permute-start.12 = (bf16[128,128]{1,0:T(8,128)(2,1)S(1)}, bf16[128,128]{1,0:T(8,128)(2,1)S(1)}, u32[]{:S(2)}, u32[]{:S(2)}) collective-permute-start(bf16[128,128]{1,0:T(8,128)(2,1)S(1)} %get-tuple-element.38), channel_id=1, source_target_pairs={{0,6},{1,7},{2,4},{3,5},{4,2},{5,3},{6,0},{7,1},{8,14},{9,15},{10,... | collective-permute-start | bytes 98312 | tf_op jit(solution)/shard_map/ppermute | solution.py:37
  44.8 4.5 %collective-permute-start.14 = (bf16[128,128]{1,0:T(8,128)(2,1)S(1)}, bf16[128,128]{1,0:T(8,128)(2,1)S(1)}, u32[]{:S(2)}, u32[]{:S(2)}) collective-permute-start(bf16[128,128]{1,0:T(8,128)(2,1)S(1)} %get-tuple-element.41), channel_id=1, source_target_pairs={{0,2},{1,3},{2,0},{3,1},{4,6},{5,7},{6,4},{7,5},{8,10},{9,11},{10,... | collective-permute-start | bytes 98312 | tf_op jit(solution)/shard_map/ppermute | solution.py:37
  44.8 4.9 %collective-permute-start.15 = (bf16[128,128]{1,0:T(8,128)(2,1)S(1)}, bf16[128,128]{1,0:T(8,128)(2,1)S(1)}, u32[]{:S(2)}, u32[]{:S(2)}) collective-permute-start(bf16[128,128]{1,0:T(8,128)(2,1)S(1)} %get-tuple-element.42), channel_id=1, source_target_pairs={{0,4},{1,5},{2,6},{3,7},{4,0},{5,1},{6,2},{7,3},{8,12},{9,13},{10,... | collective-permute-start | bytes 98312 | tf_op jit(solution)/shard_map/ppermute | solution.py:37
  46.9 5.7 %collective-permute-start.16 = (bf16[128,128]{1,0:T(8,128)(2,1)S(1)}, bf16[128,128]{1,0:T(8,128)(2,1)S(1)}, u32[]{:S(2)}, u32[]{:S(2)}) collective-permute-start(bf16[128,128]{1,0:T(8,128)(2,1)S(1)} %get-tuple-element.43), channel_id=1, source_target_pairs={{0,6},{1,7},{2,4},{3,5},{4,2},{5,3},{6,0},{7,1},{8,14},{9,15},{10,... | collective-permute-start | bytes 98312 | tf_op jit(solution)/shard_map/ppermute | solution.py:37
  49.2 10.2 %collective-permute-start.18 = (bf16[128,512]{1,0:T(8,128)(2,1)S(1)}, bf16[128,512]{1,0:T(8,128)(2,1)S(1)}, u32[]{:S(2)}, u32[]{:S(2)}) collective-permute-start(bf16[128,512]{1,0:T(8,128)(2,1)S(1)} %copy-done.6), channel_id=1, source_target_pairs={{0,8},{8,0},{16,24},{24,16},{1,9},{9,1},{17,25},{25,17},{2,10},{10... | collective-permute-start | bytes 393224 | tf_op jit(solution)/shard_map/ppermute | solution.py:37
  52.8 5.0 %collective-permute-start.21 = (bf16[128,512]{1,0:T(8,128)(2,1)S(1)}, bf16[128,512]{1,0:T(8,128)(2,1)S(1)}, u32[]{:S(2)}, u32[]{:S(2)}) collective-permute-start(bf16[128,512]{1,0:T(8,128)(2,1)S(1)} %shard_map.100.refs_4_.refs_0_), channel_id=1, source_target_pairs={{0,16},{8,24},{16,0},{24,8},{1,17},{9,25},{17,1},{25,9},{2,18},{10... | collective-permute-start | bytes 393224 | tf_op jit(solution)/shard_map/ppermute | solution.py:37
  53.6 5.9 %collective-permute-start.19 = (bf16[128,512]{1,0:T(8,128)(2,1)S(1)}, bf16[128,512]{1,0:T(8,128)(2,1)S(1)}, u32[]{:S(2)}, u32[]{:S(2)}) collective-permute-start(bf16[128,512]{1,0:T(8,128)(2,1)S(1)} %get-tuple-element.57), channel_id=1, source_target_pairs={{0,8},{8,0},{16,24},{24,16},{1,9},{9,1},{17,25},{25,17},{2,10},{10... | collective-permute-start | bytes 393224 | tf_op jit(solution)/shard_map/ppermute | solution.py:37
  53.6 5.8 %collective-permute-start.20 = (bf16[128,512]{1,0:T(8,128)(2,1)S(1)}, bf16[128,512]{1,0:T(8,128)(2,1)S(1)}, u32[]{:S(2)}, u32[]{:S(2)}) collective-permute-start(bf16[128,512]{1,0:T(8,128)(2,1)S(1)} %shard_map.100.refs_4_.refs_0_), channel_id=1, source_target_pairs={{0,8},{8,0},{16,24},{24,16},{1,9},{9,1},{17,25},{25,17},{2,10},{10... | collective-permute-start | bytes 393224 | tf_op jit(solution)/shard_map/ppermute | solution.py:37
  57.8 1.7 %collective-permute-start.22 = (bf16[128,512]{1,0:T(8,128)(2,1)S(1)}, bf16[128,512]{1,0:T(8,128)(2,1)S(1)}, u32[]{:S(2)}, u32[]{:S(2)}) collective-permute-start(bf16[128,512]{1,0:T(8,128)(2,1)S(1)} %collective-permute-done.21.refs_6_), channel_id=1, source_target_pairs={{0,8},{8,0},{16,24},{24,16},{1,9},{9,1},{17,25},{25,17},{2,10},{10... | collective-permute-start | bytes 393224 | tf_op jit(solution)/shard_map/ppermute | solution.py:37
  57.8 9.1 %collective-permute-start.17 = (bf16[4,128,256]{2,1,0:T(8,128)(2,1)S(1)}, bf16[4,128,256]{2,1,0:T(8,128)(2,1)S(1)}, u32[]{:S(2)}, u32[]{:S(2)}) collective-permute-start(bf16[4,128,256]{2,1,0:T(8,128)(2,1)S(1)} %shard_map.99), channel_id=1, source_target_pairs={{0,1},{1,0},{2,3},{3,2},{4,5},{5,4},{6,7},{7,6},{8,9},{9,8},{10,11... | collective-permute-start | bytes 786440 | tf_op jit(solution)/shard_map/ppermute | solution.py:37
  60.0 15.9 %collective-permute-start.26 = (bf16[4,64,512]{2,1,0:T(8,128)(2,1)S(1)}, bf16[4,64,512]{2,1,0:T(8,128)(2,1)S(1)}, u32[]{:S(2)}, u32[]{:S(2)}) collective-permute-start(bf16[4,64,512]{2,1,0:T(8,128)(2,1)S(1)} %get-tuple-element.52), channel_id=1, source_target_pairs={{0,1},{1,0},{2,3},{3,2},{4,5},{5,4},{6,7},{7,6},{8,9},{9,8},{10,11... | collective-permute-start | bytes 786440 | tf_op jit(solution)/shard_map/ppermute | solution.py:37
  67.0 4.5 %collective-permute-start.23 = (bf16[128,256]{1,0:T(8,128)(2,1)S(1)}, bf16[128,256]{1,0:T(8,128)(2,1)S(1)}, u32[]{:S(2)}, u32[]{:S(2)}) collective-permute-start(bf16[128,256]{1,0:T(8,128)(2,1)S(1)} %get-tuple-element.49), channel_id=1, source_target_pairs={{0,2},{1,3},{2,0},{3,1},{4,6},{5,7},{6,4},{7,5},{8,10},{9,11},{10,... | collective-permute-start | bytes 196616 | tf_op jit(solution)/shard_map/ppermute | solution.py:37
  67.0 7.5 %collective-permute-start.24 = (bf16[128,256]{1,0:T(8,128)(2,1)S(1)}, bf16[128,256]{1,0:T(8,128)(2,1)S(1)}, u32[]{:S(2)}, u32[]{:S(2)}) collective-permute-start(bf16[128,256]{1,0:T(8,128)(2,1)S(1)} %get-tuple-element.50), channel_id=1, source_target_pairs={{0,4},{1,5},{2,6},{3,7},{4,0},{5,1},{6,2},{7,3},{8,12},{9,13},{10,... | collective-permute-start | bytes 196616 | tf_op jit(solution)/shard_map/ppermute | solution.py:37
  69.9 6.1 %collective-permute-start.25 = (bf16[128,256]{1,0:T(8,128)(2,1)S(1)}, bf16[128,256]{1,0:T(8,128)(2,1)S(1)}, u32[]{:S(2)}, u32[]{:S(2)}) collective-permute-start(bf16[128,256]{1,0:T(8,128)(2,1)S(1)} %get-tuple-element.51), channel_id=1, source_target_pairs={{0,6},{1,7},{2,4},{3,5},{4,2},{5,3},{6,0},{7,1},{8,14},{9,15},{10,... | collective-permute-start | bytes 196616 | tf_op jit(solution)/shard_map/ppermute | solution.py:37
  76.0 6.8 %collective-permute-start.27 = (bf16[64,512]{1,0:T(8,128)(2,1)S(1)}, bf16[64,512]{1,0:T(8,128)(2,1)S(1)}, u32[]{:S(2)}, u32[]{:S(2)}) collective-permute-start(bf16[64,512]{1,0:T(8,128)(2,1)S(1)} %get-tuple-element.54), channel_id=1, source_target_pairs={{0,2},{1,3},{2,0},{3,1},{4,6},{5,7},{6,4},{7,5},{8,10},{9,11},{10,... | collective-permute-start | bytes 196616 | tf_op jit(solution)/shard_map/ppermute | solution.py:37
  76.1 6.7 %collective-permute-start.28 = (bf16[64,512]{1,0:T(8,128)(2,1)S(1)}, bf16[64,512]{1,0:T(8,128)(2,1)S(1)}, u32[]{:S(2)}, u32[]{:S(2)}) collective-permute-start(bf16[64,512]{1,0:T(8,128)(2,1)S(1)} %get-tuple-element.55), channel_id=1, source_target_pairs={{0,4},{1,5},{2,6},{3,7},{4,0},{5,1},{6,2},{7,3},{8,12},{9,13},{10,... | collective-permute-start | bytes 196616 | tf_op jit(solution)/shard_map/ppermute | solution.py:37
  78.3 6.1 %collective-permute-start.29 = (bf16[64,512]{1,0:T(8,128)(2,1)S(1)}, bf16[64,512]{1,0:T(8,128)(2,1)S(1)}, u32[]{:S(2)}, u32[]{:S(2)}) collective-permute-start(bf16[64,512]{1,0:T(8,128)(2,1)S(1)} %get-tuple-element.56), channel_id=1, source_target_pairs={{0,6},{1,7},{2,4},{3,5},{4,2},{5,3},{6,0},{7,1},{8,14},{9,15},{10,... | collective-permute-start | bytes 196616 | tf_op jit(solution)/shard_map/ppermute | solution.py:37
  (5 other events, 20.6 us)

commit v2 on v1

--- a/solution.py
+++ b/solution.py
@@ -39,7 +39,7 @@
 
 def call(kernel, out_shape, scratch, args, smem=0, hbm=0, after=()):
     given = len(args)
-    params = WHOLE if hbm else PARAMS
+    params = WHOLE if hbm == given else PARAMS
 
     def body(*refs):
         kernel(*refs[:given], *refs[given + len(after):])
@@ -119,18 +119,22 @@
         copy.wait()
 
 
-def hidden_kernel(fsdp, hid_ref, *rest):
-    near_refs, far_ref, sems = rest[:fsdp // 2], rest[fsdp // 2], rest[fsdp // 2 + 1]
+def hidden_moves(hid_ref, near_refs, far_ref, sems):
     mine = lax.axis_index("fsdp")
+    near = len(near_refs)
     span = far_ref.shape[2]
     copies = []
-    for m in range(fsdp):
+    for m in range(near + far_ref.shape[0]):
         columns = pl.ds(pl.multiple_of(jnp.bitwise_xor(mine, m) * span, span), span)
-        to = near_refs[m] if m < fsdp // 2 else far_ref.at[m - fsdp // 2]
+        to = near_refs[m] if m < near else far_ref.at[m - near]
         copies.append(pltpu.make_async_copy(hid_ref.at[:, columns], to, sems.at[m]))
     for copy in copies:
         copy.start()
-    for copy in copies:
+    return copies
+
+
+def hidden_kernel(hid_ref, *rest):
+    for copy in hidden_moves(hid_ref, rest[:-2], *rest[-2:]):
         copy.wait()
 
 
@@ -203,10 +207,12 @@
             stat[GROUPS + first:GROUPS + first + 1], stat[GROUPS + first + 1:GROUPS + first + 2]]
 
 
-def sequence_kernel(order_ref, *rest):
+def sequence_kernel(near_parts, order_ref, hid_ref, *rest):
     qd_refs, kv_refs, rest = rest[:TEAM], rest[TEAM:TEAM + KV_HEADS], rest[TEAM + KV_HEADS:]
     dkv_refs, keep_ref, send_ref, rest = rest[:KV_HEADS], rest[KV_HEADS], rest[KV_HEADS + 1], rest[KV_HEADS + 2:]
-    q_all, go_all, stat_all, key_all, value_all, dq_all, dkv_all = rest
+    near_refs, far_ref, rest = rest[:near_parts], rest[near_parts], rest[near_parts + 1:]
+    q_all, go_all, stat_all, key_all, value_all, dq_all, dkv_all, sems = rest
+    moves = hidden_moves(hid_ref, near_refs, far_ref, sems)
     rows = kv_refs[0].shape[0]
     head, side = head_side()
     near = [order_ref[0, 2 * jnp.bitwise_xor(head, m) + side] for m in range(KV_HEADS)]
@@ -243,6 +249,8 @@
         dkv_refs[m][...] = dkv_all[near[m]].astype(jnp.bfloat16)
         keep_ref[m] = dq_all[near[m]]
         send_ref[m] = dq_all[far[m]].astype(jnp.bfloat16)
+    for copy in moves:
+        copy.wait()
 
 
 def teams_kernel(order_ref, qd_ref, kv_ref, dkv_ref, keep_ref, send_ref, dq_all):
@@ -379,29 +387,28 @@
            pltpu.SemaphoreType.DMA((3 + 2 * KV_HEADS,))],
         (queries[0], grad_out[0], attn_out[0], log_sums[0]), hbm=4)
     qd = along_heads(qd)
-    qd = qd + [swapped(one, "ctx", 1) for one in qd]
-    *hid, hid_far = call(
-        functools.partial(hidden_kernel, fsdp), [sds((rows, span))] * far + [sds((fsdp - far, rows, span))],
-        [pltpu.SemaphoreType.DMA((fsdp,))], (inputs,), hbm=1)
-    w_far = held(swapped(w_kv, "fsdp", far), (*qd[1:KV_HEADS + 3], hid_far))
+    turned = [swapped(one, "ctx", 1) for one in qd[:2]]
+    w_far = held(swapped(w_kv, "fsdp", far), (*qd[1:KV_HEADS - 1], turned[0]))
     w_parts = over_fsdp([w_kv] * far + [w_far] * (fsdp - far), far // 2)
 
     kv = call(
         functools.partial(project_kernel, fsdp), [sds(block)] * KV_HEADS,
         [pltpu.VMEM((KV_HEADS,) + block, jnp.bfloat16)], (inputs, *w_parts))
-    kv = along_heads(kv)
-
-    hid_far = swapped(hid_far, "fsdp", far)
-    hid = over_fsdp(hid + [hid_far[m] for m in range(fsdp - far)], far // 2)
+    own_kv, kv = kv[:1], along_heads(kv)
+    late = [held(qd[2], own_kv), held(qd[3], kv[1:3])]
+    qd = qd[:2] + late + turned + [swapped(one, "ctx", 1) for one in late]
 
     half = (KV_HEADS,) + wide
+    cut = [sds((rows, span))] * far + [sds((fsdp - far, rows, span))]
+    cut_sems = pltpu.SemaphoreType.DMA((fsdp,))
     if teams == 1:
-        *dkv, keep, give = call(
-            sequence_kernel, [sds(block)] * KV_HEADS + [sds(half, f32), sds(half)],
+        outs = call(
+            functools.partial(sequence_kernel, far), [sds(block)] * KV_HEADS + [sds(half, f32), sds(half)] + cut,
             [pltpu.VMEM((TEAM,) + wide, jnp.bfloat16)] * 2 + [pltpu.VMEM((TEAM, 2 * GROUPS, rows), f32)]
             + [pltpu.VMEM((TEAM, 2 * rows, PAIR), jnp.bfloat16)] * 2
-            + [pltpu.VMEM((TEAM,) + wide, f32), pltpu.VMEM((TEAM,) + block, f32)],
-            (block_order, *qd, *kv), smem=1, after=(hid_far,))
+            + [pltpu.VMEM((TEAM,) + wide, f32), pltpu.VMEM((TEAM,) + block, f32), cut_sems],
+            (block_order, inputs, *qd, *kv), smem=1, hbm=1)
+        dkv, (keep, give, *hid, hid_far) = outs[:KV_HEADS], outs[KV_HEADS:]
     else:
         alike = [[t * TEAM + i for t in range(teams)] for i in range(TEAM)]
         kv = lax.all_gather(jnp.stack(kv), "ctx", axis_index_groups=alike, axis=0, tiled=True)
@@ -410,7 +417,10 @@
             [pltpu.VMEM((TEAM,) + wide, f32)], (block_order, jnp.stack(qd), kv), smem=1)
         dkv = lax.psum_scatter(dkv, "ctx", axis_index_groups=alike, scatter_dimension=0, tiled=True)
         dkv = [dkv[m].astype(jnp.bfloat16) for m in range(KV_HEADS)]
-
+        *hid, hid_far = call(hidden_kernel, cut, [cut_sems], (inputs,), hbm=1)
+
+    hid_far = swapped(hid_far, "fsdp", far)
+    hid = over_fsdp(hid + [hid_far[m] for m in range(fsdp - far)], far // 2)
     dkv = along_heads(dkv)
     give = swapped(held(give, dkv[1:]), "ctx", 1)
     (kv_grad,) = call(
@@ -421,7 +431,7 @@
         share = (span // devices, columns)
         own_sums, send_sums = call(
             functools.partial(sides_kernel, fsdp), [sds((KV_HEADS,) + share, f32), sds((KV_HEADS,) + share)],
-            [pltpu.VMEM((devices,) + share, f32)], (*hid, *grads))
+            [pltpu.VMEM((devices,) + share, f32)], (*hid, *grads), after=(give,))
         formed = (own_sums,)
         dq = along_heads(call(pair_kernel, [sds(wide)] * KV_HEADS, [], (keep, give), after=formed))
         sums = call(

time: 85.4 us -> 80.8 us (0.946)
  waiting for transfers between devices: 32.8 us -> 29.4 us
  Pallas kernels: 14.2 us -> 12.6 us
  starting transfers between devices: 36.2 us -> 37.6 us
  local copies, waits for them, and re-layouts: 0.99 us -> 0.04 us
    ppermute x30, waiting for transfers between devices: 32.8 us -> 29.4 us  [swapped(): return lax.ppermute(array, axis, [(i, i ^ bits) for i in range(size)])]
    pallas_call x11 -> x10, Pallas kernels: 14.2 us -> 12.6 us  [call(): pl.pallas_call(body, out_shape=out_shape, in_specs=specs, out_specs=[VMEM...]
    ppermute x30, starting transfers between devices: 36.2 us -> 37.6 us  [swapped(): return lax.ppermute(array, axis, [(i, i ^ bits) for i in range(size)])]
    unnamed x14 -> x10, local copies, waits for them, and re-layouts: 0.97 us -> 0.02 us
  transfers between devices with their start and end apart: 30 -> 30, of which waited for: 12 -> 14; matrix products, arithmetic and copies ran while one was open for 0% -> 0% of each run, Pallas kernels for 9% -> 7%
where the time goes in v2:
time: 80.8 us; the launch traced here: 80.4 us
  starting transfers between devices  37.6 us (47%)
  waiting for transfers between devices  29.4 us (36%)
  Pallas kernels  12.6 us (16%)
    ppermute x30, starting transfers between devices, swapped(): return lax.ppermute(array, axis, [(i, i ^ bits) for i in range(size)])  37.6 us
    ppermute x30, waiting for transfers between devices, swapped(): return lax.ppermute(array, axis, [(i, i ^ bits) for i in range(size)])  29.4 us
    pallas_call x10, Pallas kernels, call(): pl.pallas_call(body, out_shape=out_shape, in_specs=specs, out_specs=[VMEM...  12.6 us
  transfers between devices with their start and end apart: 30, of which 14 were waited for; matrix products, arithmetic and copies ran while one was open for 0% of the time, Pallas kernels for 7%

profile of v2, /device:TPU:0, one launch (start us, length us, event | category | flops | bytes accessed | tf_op | source)
XLA Modules:
  0.0 80.4 jit_solution(7928993789627283517)
XLA Ops:
  0.6 3.0 %collective-permute-start.3 = (bf16[512,512]{1,0:T(8,128)(2,1)}, bf16[512,512]{1,0:T(8,128)(2,1)S(1)}, u32[]{:S(2)}, u32[]{:S(2)}) collective-permute-start(bf16[512,512]{1,0:T(8,128)(2,1)} %refs_1_.3), channel_id=1, source_target_pairs={{0,16},{8,24},{16,0},{24,8},{1,17},{9,25},{17,1},{25,9},{2,18},{10... | collective-permute-start | bytes 1572872 | tf_op jit(solution)/shard_map/ppermute | solution.py:37
  3.7 2.2 %shard_map.94 = (bf16[144,512]{1,0:T(8,128)(2,1)}, bf16[144,512]{1,0:T(8,128)(2,1)}, bf16[144,512]{1,0:T(8,128)(2,1)}, bf16[144,512]{1,0:T(8,128)(2,1)}) custom-call(bf16[128,1024]{1,0:T(8,128)(2,1)} %bitcast.14, bf16[128,1024]{1,0:T(8,128)(2,1)} %bitcast.15, bf16[128,1024]{1,0:T(8,128)(2,1)} %bitcast.16, f32[16,128]{1,0:T(8,128)} %bitcast.18), custom_call_target="tpu_custom_call" | custom-call | tf_op jit(solution)/shard_map/pallas_call | solution.py:48
  5.9 1.6 %collective-permute-start = (bf16[144,512]{1,0:T(8,128)(2,1)}, bf16[144,512]{1,0:T(8,128)(2,1)S(1)}, u32[]{:S(2)}, u32[]{:S(2)}) collective-permute-start(bf16[144,512]{1,0:T(8,128)(2,1)} %get-tuple-element.31), channel_id=1, source_target_pairs={{0,2},{1,3},{2,0},{3,1},{4,6},{5,7},{6,4},{7,5},{8,10},{9,11},{10,... | collective-permute-start | bytes 442376 | tf_op jit(solution)/shard_map/ppermute | solution.py:37
  7.5 2.6 %collective-permute-start.1 = (bf16[144,512]{1,0:T(8,128)(2,1)}, bf16[144,512]{1,0:T(8,128)(2,1)S(1)}, u32[]{:S(2)}, u32[]{:S(2)}) collective-permute-start(bf16[144,512]{1,0:T(8,128)(2,1)} %get-tuple-element.32), channel_id=1, source_target_pairs={{0,4},{1,5},{2,6},{3,7},{4,0},{5,1},{6,2},{7,3},{8,12},{9,13},{10,... | collective-permute-start | bytes 442376 | tf_op jit(solution)/shard_map/ppermute | solution.py:37
  10.1 1.5 %collective-permute-start.4 = (bf16[144,512]{1,0:T(8,128)(2,1)}, bf16[144,512]{1,0:T(8,128)(2,1)S(1)}, u32[]{:S(2)}, u32[]{:S(2)}) collective-permute-start(bf16[144,512]{1,0:T(8,128)(2,1)} %get-tuple-element.30.refs_2_), channel_id=1, source_target_pairs={{0,1},{1,0},{2,3},{3,2},{4,5},{5,4},{6,7},{7,6},{8,9},{9,8},{10,11... | collective-permute-start | bytes 442376 | tf_op jit(solution)/shard_map/ppermute | solution.py:37
  11.6 2.2 %collective-permute-done.refs_1_.refs_3_ = bf16[144,512]{1,0:T(8,128)(2,1)S(1)} collective-permute-done((bf16[144,512]{1,0:T(8,128)(2,1)}, bf16[144,512]{1,0:T(8,128)(2,1)S(1)}, u32[]{:S(2)}, u32[]{:S(2)}) %collective-permute-start) | collective-permute-done | bytes 147488 | tf_op jit(solution)/shard_map/ppermute | solution.py:37
  13.9 3.0 %collective-permute-done.1.refs_2_.refs_0_ = bf16[144,512]{1,0:T(8,128)(2,1)S(1)} collective-permute-done((bf16[144,512]{1,0:T(8,128)(2,1)}, bf16[144,512]{1,0:T(8,128)(2,1)S(1)}, u32[]{:S(2)}, u32[]{:S(2)}) %collective-permute-start.1) | collective-permute-done | bytes 147488 | tf_op jit(solution)/shard_map/ppermute | solution.py:37
  17.0 2.7 %collective-permute-start.6 = (bf16[144,512]{1,0:T(8,128)(2,1)S(1)}, bf16[144,512]{1,0:T(8,128)(2,1)S(1)}, u32[]{:S(2)}, u32[]{:S(2)}) collective-permute-start(bf16[144,512]{1,0:T(8,128)(2,1)S(1)} %copy-done.4), channel_id=1, source_target_pairs={{0,6},{1,7},{2,4},{3,5},{4,2},{5,3},{6,0},{7,1},{8,14},{9,15},{10,... | collective-permute-start | bytes 442376 | tf_op jit(solution)/shard_map/ppermute | solution.py:37
  20.3 2.4 %collective-permute-start.8 = (bf16[128,128]{1,0:T(8,128)(2,1)S(1)}, bf16[128,128]{1,0:T(8,128)(2,1)S(1)}, u32[]{:S(2)}, u32[]{:S(2)}) collective-permute-start(bf16[128,128]{1,0:T(8,128)(2,1)S(1)} %get-tuple-element.36), channel_id=1, source_target_pairs={{0,4},{1,5},{2,6},{3,7},{4,0},{5,1},{6,2},{7,3},{8,12},{9,13},{10,... | collective-permute-start | bytes 98312 | tf_op jit(solution)/shard_map/ppermute | solution.py:37
  22.7 1.5 %collective-permute-start.9 = (bf16[144,512]{1,0:T(8,128)(2,1)S(1)}, bf16[144,512]{1,0:T(8,128)(2,1)S(1)}, u32[]{:S(2)}, u32[]{:S(2)}) collective-permute-start(bf16[144,512]{1,0:T(8,128)(2,1)S(1)} %collective-permute-done.refs_1_.refs_3_), channel_id=1, source_target_pairs={{0,1},{1,0},{2,3},{3,2},{4,5},{5,4},{6,7},{7,6},{8,9},{9,8},{10,11... | collective-permute-start | bytes 442376 | tf_op jit(solution)/shard_map/ppermute | solution.py:37
  24.8 0.8 %collective-permute-done.6.refs_0_ = bf16[144,512]{1,0:T(8,128)(2,1)S(1)} collective-permute-done((bf16[144,512]{1,0:T(8,128)(2,1)S(1)}, bf16[144,512]{1,0:T(8,128)(2,1)S(1)}, u32[]{:S(2)}, u32[]{:S(2)}) %collective-permute-start.6) | collective-permute-done | bytes 147488 | tf_op jit(solution)/shard_map/ppermute | solution.py:37
  25.8 2.0 %collective-permute-done.8.refs_2_.refs_12_ = bf16[128,128]{1,0:T(8,128)(2,1)S(1)} collective-permute-done((bf16[128,128]{1,0:T(8,128)(2,1)S(1)}, bf16[128,128]{1,0:T(8,128)(2,1)S(1)}, u32[]{:S(2)}, u32[]{:S(2)}) %collective-permute-start.8) | collective-permute-done | bytes 32800 | tf_op jit(solution)/shard_map/ppermute | solution.py:37
  27.9 1.5 %collective-permute-start.11 = (bf16[144,512]{1,0:T(8,128)(2,1)S(1)}, bf16[144,512]{1,0:T(8,128)(2,1)S(1)}, u32[]{:S(2)}, u32[]{:S(2)}) collective-permute-start(bf16[144,512]{1,0:T(8,128)(2,1)S(1)} %shard_map.98.refs_5_), channel_id=1, source_target_pairs={{0,1},{1,0},{2,3},{3,2},{4,5},{5,4},{6,7},{7,6},{8,9},{9,8},{10,11... | collective-permute-start | bytes 442376 | tf_op jit(solution)/shard_map/ppermute | solution.py:37
  29.4 2.5 %collective-permute-start.12 = (bf16[128,128]{1,0:T(8,128)(2,1)S(1)}, bf16[128,128]{1,0:T(8,128)(2,1)S(1)}, u32[]{:S(2)}, u32[]{:S(2)}) collective-permute-start(bf16[128,128]{1,0:T(8,128)(2,1)S(1)} %get-tuple-element.37), channel_id=1, source_target_pairs={{0,6},{1,7},{2,4},{3,5},{4,2},{5,3},{6,0},{7,1},{8,14},{9,15},{10,... | collective-permute-start | bytes 98312 | tf_op jit(solution)/shard_map/ppermute | solution.py:37
  31.8 3.2 %collective-permute-done.12.refs_13_ = bf16[128,128]{1,0:T(8,128)(2,1)S(1)} collective-permute-done((bf16[128,128]{1,0:T(8,128)(2,1)S(1)}, bf16[128,128]{1,0:T(8,128)(2,1)S(1)}, u32[]{:S(2)}, u32[]{:S(2)}) %collective-permute-start.12) | collective-permute-done | bytes 32800 | tf_op jit(solution)/shard_map/ppermute | solution.py:37
  35.1 6.0 %shard_map.99 = (bf16[128,128]{1,0:T(8,128)(2,1)S(1)}, bf16[128,128]{1,0:T(8,128)(2,1)S(1)}, bf16[128,128]{1,0:T(8,128)(2,1)S(1)}, bf16[128,128]{1,0:T(8,128)(2,...) custom-call(s32[1,8]{1,0:T(1,128)S(1)} %copy-done.3, ...), custom_call_target="tpu_custom_call" | custom-call | tf_op jit(solution)/shard_map/pallas_call | solution.py:48
  41.1 1.6 %collective-permute-start.18 = (bf16[2,128,512]{2,1,0:T(8,128)(2,1)S(1)}, bf16[2,128,512]{2,1,0:T(8,128)(2,1)S(1)}, u32[]{:S(2)}, u32[]{:S(2)}) collective-permute-start(bf16[2,128,512]{2,1,0:T(8,128)(2,1)S(1)} %get-tuple-element.45), channel_id=1, source_target_pairs={{0,16},{8,24},{16,0},{24,8},{1,17},{9,25},{17,1},{25,9},{2,18},{10... | collective-permute-start | bytes 786440 | tf_op jit(solution)/shard_map/ppermute | solution.py:37
  42.7 3.0 %collective-permute-start.14 = (bf16[128,128]{1,0:T(8,128)(2,1)S(1)}, bf16[128,128]{1,0:T(8,128)(2,1)S(1)}, u32[]{:S(2)}, u32[]{:S(2)}) collective-permute-start(bf16[128,128]{1,0:T(8,128)(2,1)S(1)} %get-tuple-element.41), channel_id=1, source_target_pairs={{0,4},{1,5},{2,6},{3,7},{4,0},{5,1},{6,2},{7,3},{8,12},{9,13},{10,... | collective-permute-start | bytes 98312 | tf_op jit(solution)/shard_map/ppermute | solution.py:37
  45.8 1.3 %collective-permute-start.15 = (bf16[128,128]{1,0:T(8,128)(2,1)S(1)}, bf16[128,128]{1,0:T(8,128)(2,1)S(1)}, u32[]{:S(2)}, u32[]{:S(2)}) collective-permute-start(bf16[128,128]{1,0:T(8,128)(2,1)S(1)} %get-tuple-element.42), channel_id=1, source_target_pairs={{0,6},{1,7},{2,4},{3,5},{4,2},{5,3},{6,0},{7,1},{8,14},{9,15},{10,... | collective-permute-start | bytes 98312 | tf_op jit(solution)/shard_map/ppermute | solution.py:37
  47.7 3.8 %collective-permute-done.15.refs_3_ = bf16[128,128]{1,0:T(8,128)(2,1)S(1)} collective-permute-done((bf16[128,128]{1,0:T(8,128)(2,1)S(1)}, bf16[128,128]{1,0:T(8,128)(2,1)S(1)}, u32[]{:S(2)}, u32[]{:S(2)}) %collective-permute-start.15) | collective-permute-done | bytes 32800 | tf_op jit(solution)/shard_map/ppermute | solution.py:37
  53.2 3.4 %collective-permute-done.21.refs_6_ = bf16[128,512]{1,0:T(8,128)(2,1)S(1)} collective-permute-done((bf16[128,512]{1,0:T(8,128)(2,1)S(1)}, bf16[128,512]{1,0:T(8,128)(2,1)S(1)}, u32[]{:S(2)}, u32[]{:S(2)}) %collective-permute-start.21) | collective-permute-done | bytes 131104 | tf_op jit(solution)/shard_map/ppermute | solution.py:37
  57.2 0.7 collective-permute-done.22.refs_7_
  58.0 2.9 %collective-permute-done.16.refs_8_.refs_1_ = bf16[4,128,256]{2,1,0:T(8,128)(2,1)S(1)} collective-permute-done((bf16[4,128,256]{2,1,0:T(8,128)(2,1)S(1)}, bf16[4,128,256]{2,1,0:T(8,128)(2,1)S(1)}, u32[]{:S(2)}, u32[]{:S(2)}) %collective-permute-start.16) | collective-permute-done | bytes 262176 | tf_op jit(solution)/shard_map/ppermute | solution.py:37
  62.2 2.1 %collective-permute-start.24 = (bf16[128,256]{1,0:T(8,128)(2,1)S(1)}, bf16[128,256]{1,0:T(8,128)(2,1)S(1)}, u32[]{:S(2)}, u32[]{:S(2)}) collective-permute-start(bf16[128,256]{1,0:T(8,128)(2,1)S(1)} %get-tuple-element.50), channel_id=1, source_target_pairs={{0,4},{1,5},{2,6},{3,7},{4,0},{5,1},{6,2},{7,3},{8,12},{9,13},{10,... | collective-permute-start | bytes 196616 | tf_op jit(solution)/shard_map/ppermute | solution.py:37
  64.3 2.3 %collective-permute-start.25 = (bf16[128,256]{1,0:T(8,128)(2,1)S(1)}, bf16[128,256]{1,0:T(8,128)(2,1)S(1)}, u32[]{:S(2)}, u32[]{:S(2)}) collective-permute-start(bf16[128,256]{1,0:T(8,128)(2,1)S(1)} %get-tuple-element.51), channel_id=1, source_target_pairs={{0,6},{1,7},{2,4},{3,5},{4,2},{5,3},{6,0},{7,1},{8,14},{9,15},{10,... | collective-permute-start | bytes 196616 | tf_op jit(solution)/shard_map/ppermute | solution.py:37
  66.5 2.3 %collective-permute-done.24.refs_2_.refs_3_ = bf16[128,256]{1,0:T(8,128)(2,1)S(1)} collective-permute-done((bf16[128,256]{1,0:T(8,128)(2,1)S(1)}, bf16[128,256]{1,0:T(8,128)(2,1)S(1)}, u32[]{:S(2)}, u32[]{:S(2)}) %collective-permute-start.24) | collective-permute-done | bytes 65568 | tf_op jit(solution)/shard_map/ppermute | solution.py:37
  68.8 1.6 %collective-permute-done.25.refs_3_.refs_4_ = bf16[128,256]{1,0:T(8,128)(2,1)S(1)} collective-permute-done((bf16[128,256]{1,0:T(8,128)(2,1)S(1)}, bf16[128,256]{1,0:T(8,128)(2,1)S(1)}, u32[]{:S(2)}, u32[]{:S(2)}) %collective-permute-start.25) | collective-permute-done | bytes 65568 | tf_op jit(solution)/shard_map/ppermute | solution.py:37
  70.5 3.2 %collective-permute-start.28 = (bf16[64,512]{1,0:T(8,128)(2,1)S(1)}, bf16[64,512]{1,0:T(8,128)(2,1)S(1)}, u32[]{:S(2)}, u32[]{:S(2)}) collective-permute-start(bf16[64,512]{1,0:T(8,128)(2,1)S(1)} %get-tuple-element.55), channel_id=1, source_target_pairs={{0,4},{1,5},{2,6},{3,7},{4,0},{5,1},{6,2},{7,3},{8,12},{9,13},{10,... | collective-permute-start | bytes 196616 | tf_op jit(solution)/shard_map/ppermute | solution.py:37
  73.7 1.2 %collective-permute-start.29 = (bf16[64,512]{1,0:T(8,128)(2,1)S(1)}, bf16[64,512]{1,0:T(8,128)(2,1)S(1)}, u32[]{:S(2)}, u32[]{:S(2)}) collective-permute-start(bf16[64,512]{1,0:T(8,128)(2,1)S(1)} %get-tuple-element.56), channel_id=1, source_target_pairs={{0,6},{1,7},{2,4},{3,5},{4,2},{5,3},{6,0},{7,1},{8,14},{9,15},{10,... | collective-permute-start | bytes 196616 | tf_op jit(solution)/shard_map/ppermute | solution.py:37
  74.9 1.6 %shard_map.105 = bf16[128,2048]{1,0:T(8,128)(2,1)} custom-call(bf16[128,512]{1,0:T(8,128)(2,1)S(1)} %shard_map.101.refs_4_.refs_0_, bf16[512,512]{1,0:T(8,128)(2,1)S(1)} %copy-done, bf16[512,512]{1,0:T(8,128)(2,1)S(1)} %collective-permute-done.2.refs_2_, bf16[512,512]{1,0:T(8,128)(2,1)S(1)} %shard_map.95.refs_3_, ...), custom_call_target="tpu_custom_call" | custom-call | tf_op jit(solution)/shard_map/pallas_call | solution.py:48
  76.5 0.7 shard_map.104
  77.2 2.5 %collective-permute-done.29.refs_3_ = bf16[64,512]{1,0:T(8,128)(2,1)S(1)} collective-permute-done((bf16[64,512]{1,0:T(8,128)(2,1)S(1)}, bf16[64,512]{1,0:T(8,128)(2,1)S(1)}, u32[]{:S(2)}, u32[]{:S(2)}) %collective-permute-start.29) | collective-permute-done | bytes 65568 | tf_op jit(solution)/shard_map/ppermute | solution.py:37
  (53 shorter events, 6.4 us)
Async XLA Ops:
  0.6 11.0 %copy-start = (bf16[512,512]{1,0:T(8,128)(2,1)S(1)}, bf16[512,512]{1,0:T(8,128)(2,1)}, u32[]{:S(2)}) copy-start(bf16[512,512]{1,0:T(8,128)(2,1)} %refs_1_.3) | copy-start | bytes 1572868
  0.6 16.3 %collective-permute-start.3 = (bf16[512,512]{1,0:T(8,128)(2,1)}, bf16[512,512]{1,0:T(8,128)(2,1)S(1)}, u32[]{:S(2)}, u32[]{:S(2)}) collective-permute-start(bf16[512,512]{1,0:T(8,128)(2,1)} %refs_1_.3), channel_id=1, source_target_pairs={{0,16},{8,24},{16,0},{24,8},{1,17},{9,25},{17,1},{25,9},{2,18},{10... | collective-permute-start | bytes 1572872 | tf_op jit(solution)/shard_map/ppermute | solution.py:37
  5.9 8.0 %collective-permute-start = (bf16[144,512]{1,0:T(8,128)(2,1)}, bf16[144,512]{1,0:T(8,128)(2,1)S(1)}, u32[]{:S(2)}, u32[]{:S(2)}) collective-permute-start(bf16[144,512]{1,0:T(8,128)(2,1)} %get-tuple-element.31), channel_id=1, source_target_pairs={{0,2},{1,3},{2,0},{3,1},{4,6},{5,7},{6,4},{7,5},{8,10},{9,11},{10,... | collective-permute-start | bytes 442376 | tf_op jit(solution)/shard_map/ppermute | solution.py:37
  7.5 9.3 %collective-permute-start.1 = (bf16[144,512]{1,0:T(8,128)(2,1)}, bf16[144,512]{1,0:T(8,128)(2,1)S(1)}, u32[]{:S(2)}, u32[]{:S(2)}) collective-permute-start(bf16[144,512]{1,0:T(8,128)(2,1)} %get-tuple-element.32), channel_id=1, source_target_pairs={{0,4},{1,5},{2,6},{3,7},{4,0},{5,1},{6,2},{7,3},{8,12},{9,13},{10,... | collective-permute-start | bytes 442376 | tf_op jit(solution)/shard_map/ppermute | solution.py:37
  10.1 6.8 %collective-permute-start.4 = (bf16[144,512]{1,0:T(8,128)(2,1)}, bf16[144,512]{1,0:T(8,128)(2,1)S(1)}, u32[]{:S(2)}, u32[]{:S(2)}) collective-permute-start(bf16[144,512]{1,0:T(8,128)(2,1)} %get-tuple-element.30.refs_2_), channel_id=1, source_target_pairs={{0,1},{1,0},{2,3},{3,2},{4,5},{5,4},{6,7},{7,6},{8,9},{9,8},{10,11... | collective-permute-start | bytes 442376 | tf_op jit(solution)/shard_map/ppermute | solution.py:37
  11.6 8.0 %collective-permute-start.2 = (bf16[512,512]{1,0:T(8,128)(2,1)S(1)}, bf16[512,512]{1,0:T(8,128)(2,1)S(1)}, u32[]{:S(2)}, u32[]{:S(2)}) collective-permute-start(bf16[512,512]{1,0:T(8,128)(2,1)S(1)} %copy-done), channel_id=1, source_target_pairs={{0,8},{8,0},{16,24},{24,16},{1,9},{9,1},{17,25},{25,17},{2,10},{10... | collective-permute-start | bytes 1572872 | tf_op jit(solution)/shard_map/ppermute | solution.py:37
  16.9 2.8 %collective-permute-start.5 = (bf16[512,512]{1,0:T(8,128)(2,1)S(1)}, bf16[512,512]{1,0:T(8,128)(2,1)S(1)}, u32[]{:S(2)}, u32[]{:S(2)}) collective-permute-start(bf16[512,512]{1,0:T(8,128)(2,1)S(1)} %shard_map.95.refs_3_), channel_id=1, source_target_pairs={{0,8},{8,0},{16,24},{24,16},{1,9},{9,1},{17,25},{25,17},{2,10},{10... | collective-permute-start | bytes 1572872 | tf_op jit(solution)/shard_map/ppermute | solution.py:37
  17.0 8.6 %collective-permute-start.6 = (bf16[144,512]{1,0:T(8,128)(2,1)S(1)}, bf16[144,512]{1,0:T(8,128)(2,1)S(1)}, u32[]{:S(2)}, u32[]{:S(2)}) collective-permute-start(bf16[144,512]{1,0:T(8,128)(2,1)S(1)} %copy-done.4), channel_id=1, source_target_pairs={{0,6},{1,7},{2,4},{3,5},{4,2},{5,3},{6,0},{7,1},{8,14},{9,15},{10,... | collective-permute-start | bytes 442376 | tf_op jit(solution)/shard_map/ppermute | solution.py:37
  20.2 5.6 %collective-permute-start.7 = (bf16[128,128]{1,0:T(8,128)(2,1)S(1)}, bf16[128,128]{1,0:T(8,128)(2,1)S(1)}, u32[]{:S(2)}, u32[]{:S(2)}) collective-permute-start(bf16[128,128]{1,0:T(8,128)(2,1)S(1)} %get-tuple-element.35), channel_id=1, source_target_pairs={{0,2},{1,3},{2,0},{3,1},{4,6},{5,7},{6,4},{7,5},{8,10},{9,11},{10,... | collective-permute-start | bytes 98312 | tf_op jit(solution)/shard_map/ppermute | solution.py:37
  20.3 7.6 %collective-permute-start.8 = (bf16[128,128]{1,0:T(8,128)(2,1)S(1)}, bf16[128,128]{1,0:T(8,128)(2,1)S(1)}, u32[]{:S(2)}, u32[]{:S(2)}) collective-permute-start(bf16[128,128]{1,0:T(8,128)(2,1)S(1)} %get-tuple-element.36), channel_id=1, source_target_pairs={{0,4},{1,5},{2,6},{3,7},{4,0},{5,1},{6,2},{7,3},{8,12},{9,13},{10,... | collective-permute-start | bytes 98312 | tf_op jit(solution)/shard_map/ppermute | solution.py:37
  22.7 9.1 %collective-permute-start.9 = (bf16[144,512]{1,0:T(8,128)(2,1)S(1)}, bf16[144,512]{1,0:T(8,128)(2,1)S(1)}, u32[]{:S(2)}, u32[]{:S(2)}) collective-permute-start(bf16[144,512]{1,0:T(8,128)(2,1)S(1)} %collective-permute-done.refs_1_.refs_3_), channel_id=1, source_target_pairs={{0,1},{1,0},{2,3},{3,2},{4,5},{5,4},{6,7},{7,6},{8,9},{9,8},{10,11... | collective-permute-start | bytes 442376 | tf_op jit(solution)/shard_map/ppermute | solution.py:37
  24.2 10.9 %copy-start.2 = (bf16[144,512]{1,0:T(8,128)(2,1)S(1)}, bf16[144,512]{1,0:T(8,128)(2,1)}, u32[]{:S(2)}) copy-start(bf16[144,512]{1,0:T(8,128)(2,1)} %get-tuple-element.30.refs_2_) | copy-start | bytes 442372
  24.2 10.9 %collective-permute-start.10 = (bf16[144,512]{1,0:T(8,128)(2,1)S(1)}, bf16[144,512]{1,0:T(8,128)(2,1)S(1)}, u32[]{:S(2)}, u32[]{:S(2)}) collective-permute-start(bf16[144,512]{1,0:T(8,128)(2,1)S(1)} %shard_map.97.refs_4_), channel_id=1, source_target_pairs={{0,1},{1,0},{2,3},{3,2},{4,5},{5,4},{6,7},{7,6},{8,9},{9,8},{10,11... | collective-permute-start | bytes 442376 | tf_op jit(solution)/shard_map/ppermute | solution.py:37
  27.9 7.2 %collective-permute-start.11 = (bf16[144,512]{1,0:T(8,128)(2,1)S(1)}, bf16[144,512]{1,0:T(8,128)(2,1)S(1)}, u32[]{:S(2)}, u32[]{:S(2)}) collective-permute-start(bf16[144,512]{1,0:T(8,128)(2,1)S(1)} %shard_map.98.refs_5_), channel_id=1, source_target_pairs={{0,1},{1,0},{2,3},{3,2},{4,5},{5,4},{6,7},{7,6},{8,9},{9,8},{10,11... | collective-permute-start | bytes 442376 | tf_op jit(solution)/shard_map/ppermute | solution.py:37
  29.4 5.7 %collective-permute-start.12 = (bf16[128,128]{1,0:T(8,128)(2,1)S(1)}, bf16[128,128]{1,0:T(8,128)(2,1)S(1)}, u32[]{:S(2)}, u32[]{:S(2)}) collective-permute-start(bf16[128,128]{1,0:T(8,128)(2,1)S(1)} %get-tuple-element.37), channel_id=1, source_target_pairs={{0,6},{1,7},{2,4},{3,5},{4,2},{5,3},{6,0},{7,1},{8,14},{9,15},{10,... | collective-permute-start | bytes 98312 | tf_op jit(solution)/shard_map/ppermute | solution.py:37
  41.1 15.5 %collective-permute-start.18 = (bf16[2,128,512]{2,1,0:T(8,128)(2,1)S(1)}, bf16[2,128,512]{2,1,0:T(8,128)(2,1)S(1)}, u32[]{:S(2)}, u32[]{:S(2)}) collective-permute-start(bf16[2,128,512]{2,1,0:T(8,128)(2,1)S(1)} %get-tuple-element.45), channel_id=1, source_target_pairs={{0,16},{8,24},{16,0},{24,8},{1,17},{9,25},{17,1},{25,9},{2,18},{10... | collective-permute-start | bytes 786440 | tf_op jit(solution)/shard_map/ppermute | solution.py:37
  42.7 4.4 %collective-permute-start.13 = (bf16[128,128]{1,0:T(8,128)(2,1)S(1)}, bf16[128,128]{1,0:T(8,128)(2,1)S(1)}, u32[]{:S(2)}, u32[]{:S(2)}) collective-permute-start(bf16[128,128]{1,0:T(8,128)(2,1)S(1)} %get-tuple-element.40), channel_id=1, source_target_pairs={{0,2},{1,3},{2,0},{3,1},{4,6},{5,7},{6,4},{7,5},{8,10},{9,11},{10,... | collective-permute-start | bytes 98312 | tf_op jit(solution)/shard_map/ppermute | solution.py:37
  42.7 4.9 %collective-permute-start.14 = (bf16[128,128]{1,0:T(8,128)(2,1)S(1)}, bf16[128,128]{1,0:T(8,128)(2,1)S(1)}, u32[]{:S(2)}, u32[]{:S(2)}) collective-permute-start(bf16[128,128]{1,0:T(8,128)(2,1)S(1)} %get-tuple-element.41), channel_id=1, source_target_pairs={{0,4},{1,5},{2,6},{3,7},{4,0},{5,1},{6,2},{7,3},{8,12},{9,13},{10,... | collective-permute-start | bytes 98312 | tf_op jit(solution)/shard_map/ppermute | solution.py:37
  45.8 5.7 %collective-permute-start.15 = (bf16[128,128]{1,0:T(8,128)(2,1)S(1)}, bf16[128,128]{1,0:T(8,128)(2,1)S(1)}, u32[]{:S(2)}, u32[]{:S(2)}) collective-permute-start(bf16[128,128]{1,0:T(8,128)(2,1)S(1)} %get-tuple-element.42), channel_id=1, source_target_pairs={{0,6},{1,7},{2,4},{3,5},{4,2},{5,3},{6,0},{7,1},{8,14},{9,15},{10,... | collective-permute-start | bytes 98312 | tf_op jit(solution)/shard_map/ppermute | solution.py:37
  51.6 5.0 %collective-permute-start.21 = (bf16[128,512]{1,0:T(8,128)(2,1)S(1)}, bf16[128,512]{1,0:T(8,128)(2,1)S(1)}, u32[]{:S(2)}, u32[]{:S(2)}) collective-permute-start(bf16[128,512]{1,0:T(8,128)(2,1)S(1)} %shard_map.101.refs_4_.refs_0_), channel_id=1, source_target_pairs={{0,16},{8,24},{16,0},{24,8},{1,17},{9,25},{17,1},{25,9},{2,18},{10... | collective-permute-start | bytes 393224 | tf_op jit(solution)/shard_map/ppermute | solution.py:37
  52.2 5.1 %collective-permute-start.17 = (bf16[128,512]{1,0:T(8,128)(2,1)S(1)}, bf16[128,512]{1,0:T(8,128)(2,1)S(1)}, u32[]{:S(2)}, u32[]{:S(2)}) collective-permute-start(bf16[128,512]{1,0:T(8,128)(2,1)S(1)} %get-tuple-element.44), channel_id=1, source_target_pairs={{0,8},{8,0},{16,24},{24,16},{1,9},{9,1},{17,25},{25,17},{2,10},{10... | collective-permute-start | bytes 393224 | tf_op jit(solution)/shard_map/ppermute | solution.py:37
  52.2 5.1 %collective-permute-start.20 = (bf16[128,512]{1,0:T(8,128)(2,1)S(1)}, bf16[128,512]{1,0:T(8,128)(2,1)S(1)}, u32[]{:S(2)}, u32[]{:S(2)}) collective-permute-start(bf16[128,512]{1,0:T(8,128)(2,1)S(1)} %shard_map.101.refs_4_.refs_0_), channel_id=1, source_target_pairs={{0,8},{8,0},{16,24},{24,16},{1,9},{9,1},{17,25},{25,17},{2,10},{10... | collective-permute-start | bytes 393224 | tf_op jit(solution)/shard_map/ppermute | solution.py:37
  52.7 8.2 %collective-permute-start.16 = (bf16[4,128,256]{2,1,0:T(8,128)(2,1)S(1)}, bf16[4,128,256]{2,1,0:T(8,128)(2,1)S(1)}, u32[]{:S(2)}, u32[]{:S(2)}) collective-permute-start(bf16[4,128,256]{2,1,0:T(8,128)(2,1)S(1)} %shard_map.100), channel_id=1, source_target_pairs={{0,1},{1,0},{2,3},{3,2},{4,5},{5,4},{6,7},{7,6},{8,9},{9,8},{10,11... | collective-permute-start | bytes 786440 | tf_op jit(solution)/shard_map/ppermute | solution.py:37
  56.6 1.3 %collective-permute-start.22 = (bf16[128,512]{1,0:T(8,128)(2,1)S(1)}, bf16[128,512]{1,0:T(8,128)(2,1)S(1)}, u32[]{:S(2)}, u32[]{:S(2)}) collective-permute-start(bf16[128,512]{1,0:T(8,128)(2,1)S(1)} %collective-permute-done.21.refs_6_), channel_id=1, source_target_pairs={{0,8},{8,0},{16,24},{24,16},{1,9},{9,1},{17,25},{25,17},{2,10},{10... | collective-permute-start | bytes 393224 | tf_op jit(solution)/shard_map/ppermute | solution.py:37
  56.7 4.2 %collective-permute-start.19 = (bf16[128,512]{1,0:T(8,128)(2,1)S(1)}, bf16[128,512]{1,0:T(8,128)(2,1)S(1)}, u32[]{:S(2)}, u32[]{:S(2)}) collective-permute-start(bf16[128,512]{1,0:T(8,128)(2,1)S(1)} %get-tuple-element.57), channel_id=1, source_target_pairs={{0,8},{8,0},{16,24},{24,16},{1,9},{9,1},{17,25},{25,17},{2,10},{10... | collective-permute-start | bytes 393224 | tf_op jit(solution)/shard_map/ppermute | solution.py:37
  61.4 8.9 %collective-permute-start.26 = (bf16[4,64,512]{2,1,0:T(8,128)(2,1)S(1)}, bf16[4,64,512]{2,1,0:T(8,128)(2,1)S(1)}, u32[]{:S(2)}, u32[]{:S(2)}) collective-permute-start(bf16[4,64,512]{2,1,0:T(8,128)(2,1)S(1)} %get-tuple-element.52), channel_id=1, source_target_pairs={{0,1},{1,0},{2,3},{3,2},{4,5},{5,4},{6,7},{7,6},{8,9},{9,8},{10,11... | collective-permute-start | bytes 786440 | tf_op jit(solution)/shard_map/ppermute | solution.py:37
  62.1 4.5 %collective-permute-start.23 = (bf16[128,256]{1,0:T(8,128)(2,1)S(1)}, bf16[128,256]{1,0:T(8,128)(2,1)S(1)}, u32[]{:S(2)}, u32[]{:S(2)}) collective-permute-start(bf16[128,256]{1,0:T(8,128)(2,1)S(1)} %get-tuple-element.49), channel_id=1, source_target_pairs={{0,2},{1,3},{2,0},{3,1},{4,6},{5,7},{6,4},{7,5},{8,10},{9,11},{10,... | collective-permute-start | bytes 196616 | tf_op jit(solution)/shard_map/ppermute | solution.py:37
  62.2 6.6 %collective-permute-start.24 = (bf16[128,256]{1,0:T(8,128)(2,1)S(1)}, bf16[128,256]{1,0:T(8,128)(2,1)S(1)}, u32[]{:S(2)}, u32[]{:S(2)}) collective-permute-start(bf16[128,256]{1,0:T(8,128)(2,1)S(1)} %get-tuple-element.50), channel_id=1, source_target_pairs={{0,4},{1,5},{2,6},{3,7},{4,0},{5,1},{6,2},{7,3},{8,12},{9,13},{10,... | collective-permute-start | bytes 196616 | tf_op jit(solution)/shard_map/ppermute | solution.py:37
  64.3 6.1 %collective-permute-start.25 = (bf16[128,256]{1,0:T(8,128)(2,1)S(1)}, bf16[128,256]{1,0:T(8,128)(2,1)S(1)}, u32[]{:S(2)}, u32[]{:S(2)}) collective-permute-start(bf16[128,256]{1,0:T(8,128)(2,1)S(1)} %get-tuple-element.51), channel_id=1, source_target_pairs={{0,6},{1,7},{2,4},{3,5},{4,2},{5,3},{6,0},{7,1},{8,14},{9,15},{10,... | collective-permute-start | bytes 196616 | tf_op jit(solution)/shard_map/ppermute | solution.py:37
  70.4 6.8 %collective-permute-start.27 = (bf16[64,512]{1,0:T(8,128)(2,1)S(1)}, bf16[64,512]{1,0:T(8,128)(2,1)S(1)}, u32[]{:S(2)}, u32[]{:S(2)}) collective-permute-start(bf16[64,512]{1,0:T(8,128)(2,1)S(1)} %get-tuple-element.54), channel_id=1, source_target_pairs={{0,2},{1,3},{2,0},{3,1},{4,6},{5,7},{6,4},{7,5},{8,10},{9,11},{10,... | collective-permute-start | bytes 196616 | tf_op jit(solution)/shard_map/ppermute | solution.py:37
  70.5 6.7 %collective-permute-start.28 = (bf16[64,512]{1,0:T(8,128)(2,1)S(1)}, bf16[64,512]{1,0:T(8,128)(2,1)S(1)}, u32[]{:S(2)}, u32[]{:S(2)}) collective-permute-start(bf16[64,512]{1,0:T(8,128)(2,1)S(1)} %get-tuple-element.55), channel_id=1, source_target_pairs={{0,4},{1,5},{2,6},{3,7},{4,0},{5,1},{6,2},{7,3},{8,12},{9,13},{10,... | collective-permute-start | bytes 196616 | tf_op jit(solution)/shard_map/ppermute | solution.py:37
  73.7 6.1 %collective-permute-start.29 = (bf16[64,512]{1,0:T(8,128)(2,1)S(1)}, bf16[64,512]{1,0:T(8,128)(2,1)S(1)}, u32[]{:S(2)}, u32[]{:S(2)}) collective-permute-start(bf16[64,512]{1,0:T(8,128)(2,1)S(1)} %get-tuple-element.56), channel_id=1, source_target_pairs={{0,6},{1,7},{2,4},{3,5},{4,2},{5,3},{6,0},{7,1},{8,14},{9,15},{10,... | collective-permute-start | bytes 196616 | tf_op jit(solution)/shard_map/ppermute | solution.py:37
  (3 other events, 23.6 us)
